TPU v7x, 128 devices: a whole 4x4x4 slice. The times are simulated.
128 devices in a mesh: dp: 16 (over y, z_hi, core), expert: 8 (over z_lo, x).
Axes of the slice: x: 4, y: 4, z: 4 (z_hi: 2, z_lo: 2; z = z_hi * 2 + z_lo), core: 2. Of those that a mesh axis runs over, the one named last changes fastest.
Arguments:
- policy_hidden: bfloat16 [2048, 4096], P('dp', 'expert'), may hold values from -6 to 6
- reference_hidden: bfloat16 [2048, 4096], P('dp', 'expert'), may hold values from -6 to 6
- policy_norm_gain: float32 [4096], P('expert'), may hold values from 0.25 to 1.75
- reference_norm_gain: float32 [4096], P('expert'), may hold values from 0.25 to 1.75
- policy_router: float32 [4096, 8], P('expert'), may hold values from -5.1875 to 5.1875
- reference_router: float32 [4096, 8], P('expert'), may hold values from -5.1875 to 5.1875
- policy_gate: bfloat16 [8, 4096, 8192], P('expert', 'dp'), may hold values from -0.09375 to 0.09375
- policy_up: bfloat16 [8, 4096, 8192], P('expert', 'dp'), may hold values from -0.09375 to 0.09375
- policy_down: bfloat16 [8, 8192, 4096], P('expert', 'dp'), may hold values from -0.0625 to 0.0625
- reference_gate: bfloat16 [8, 4096, 8192], P('expert', 'dp'), may hold values from -0.09375 to 0.09375
- reference_up: bfloat16 [8, 4096, 8192], P('expert', 'dp'), may hold values from -0.09375 to 0.09375
- reference_down: bfloat16 [8, 8192, 4096], P('expert', 'dp'), may hold values from -0.0625 to 0.0625
- expert_ids: int32 [2048, 2], P('dp'), may hold values from 0 to 7, all different within a row; in each aligned block of 128 rows (0 to 127, 128 to 255, ...) at most 48 rows name the same one
- lengths: int32 [64], P('dp'), may hold values from 1 to 32, as said below
Outputs:
- policy_mixture: bfloat16 [2048, 4096], P('dp', 'expert')
- reference_mixture: bfloat16 [2048, 4096], P('dp', 'expert')
- token_kl: float32 [2048], P('dp')
- loss: float32 [], replicated
Inputs may be any that keep to these rules, and one draw needn't show every extreme that they name: `expert_ids`: each row names 2 different experts; among the rows of one index of dp (aligned blocks of 128 rows) no expert is named more than 48 times, and in some block one expert is named exactly 48 times. The first lengths[r] of rollout r's 32 positions are live.
All inputs are finite; a program needn't handle non-finite values.
Results may differ from a plain program's by a relative error of at most 0.02.
Values may be sent and summed in bfloat16 or wider, within the bound.
No kernel may reach another device: no remote copies, remote signals or barrier semaphores. Data moves between devices by JAX's collectives and lax.ppermute only.
A program may use at most 256 MiB of HBM per device.

v0:
```python
import jax
import jax.numpy as jnp
from jax import lax
from jax.sharding import Mesh
from jax.sharding import PartitionSpec as P

D = 4096
SEG = 32
DP = ("dp_0", "dp_1", "dp_2")


EPSILON = 1e-05
KL_WEIGHT = 1.0
BALANCE_WEIGHT = 0.5


def cut_along(value, dim, peers):
    before, after = (value.shape[:dim], value.shape[dim + 1 :])
    return jnp.moveaxis(value.reshape(*before, peers, -1, *after), dim, 0)


def sum_by_chip(value, chips, core, dim):
    sizes = (lax.axis_size(chips), lax.axis_size(core))
    tiles = cut_along(value, dim, sizes[0] * sizes[1])
    inside = tiles.shape[1:]
    tiles = tiles.reshape(*sizes, *inside).swapaxes(0, 1).reshape(-1, *inside)
    tiles = lax.psum_scatter(tiles, core, scatter_dimension=0, tiled=True)
    return lax.psum_scatter(tiles, chips, scatter_dimension=0, tiled=True)[0]


def from_everyone(value, axis):
    copies = jnp.broadcast_to(value, (lax.axis_size(axis), *value.shape))
    return lax.all_to_all(copies, axis, split_axis=0, concat_axis=0, tiled=True)


def of_everyone(value, axis):
    return from_everyone(value, axis).sum(axis=0)


def together(arrays, axis):
    ends = [0]
    for a in arrays:
        ends.append(ends[-1] + a.size)
    so_far = of_everyone(jnp.concatenate([a.ravel() for a in arrays]), axis)
    return tuple((so_far[b:e].reshape(a.shape) for a, b, e in zip(arrays, ends, ends[1:])))


def sent_together(arrays, axis, split_dim, concat_dim, along):
    widths = [a.shape[along] for a in arrays]
    both = jnp.concatenate(arrays, axis=along)
    whole = lax.all_to_all(both, axis, split_axis=split_dim, concat_axis=concat_dim, tiled=True)
    return tuple(jnp.split(whole, [sum(widths[:k]) for k in range(1, len(widths))], axis=along))


def router_terms(hidden, norm_gain, router):
    values = hidden.astype(jnp.float32)
    partial_logits = jnp.dot(values * norm_gain, router, precision=lax.Precision.HIGHEST)
    return (partial_logits, jnp.sum(values * values, axis=1))


def expert_terms(piece_rows, weights):
    results = []
    for model_index in range(len(weights)):
        gate_weight, up_weight, down_weight = weights[model_index]
        model_rows = piece_rows[:, model_index, :]
        gate_value = jnp.dot(model_rows, gate_weight, preferred_element_type=jnp.float32)
        up_value = jnp.dot(model_rows, up_weight, preferred_element_type=jnp.float32)
        hidden = (jax.nn.silu(gate_value) * up_value).astype(jnp.bfloat16)
        results.append(jnp.dot(hidden, down_weight, preferred_element_type=jnp.float32))
    return jnp.stack(results, axis=1)


def mixture(slot_rows, weights):
    expert_count, slot_count, models, feature_block = slot_rows.shape
    model_width = expert_count * feature_block
    arrived_rows = lax.all_to_all(slot_rows, "expert", split_axis=0, concat_axis=3, tiled=True)
    local_rows = arrived_rows.reshape(slot_count, models, model_width)
    partial_terms = expert_terms(
        lax.all_gather(local_rows, DP, axis=0, tiled=True), weights
    ).astype(jnp.bfloat16)
    summed = (
        sum_by_chip(partial_terms, ("dp_0", "dp_1"), "dp_2", 0)
        .astype(jnp.float32)
        .astype(jnp.bfloat16)
    )
    result = lax.all_to_all(
        summed.reshape(1, slot_count, models, model_width),
        "expert",
        split_axis=3,
        concat_axis=0,
        tiled=True,
    )
    return result


def per_device(
    policy_hidden,
    reference_hidden,
    policy_norm_gain,
    reference_norm_gain,
    policy_router,
    reference_router,
    policy_gate,
    policy_up,
    policy_down,
    reference_gate,
    reference_up,
    reference_down,
    expert_ids,
    lengths,
):
    expert_count = lax.axis_size("expert")
    token_count, feature_block = policy_hidden.shape
    route_count = expert_ids.shape[1]
    slot_count = 3 * token_count // expert_count
    token_total = float(token_count * lax.axis_size(DP))
    policy_partial, policy_squares = router_terms(policy_hidden, policy_norm_gain, policy_router)
    reference_partial, reference_squares = router_terms(
        reference_hidden, reference_norm_gain, reference_router
    )
    policy_partial, reference_partial, policy_squares, reference_squares = together(
        (policy_partial, reference_partial, policy_squares, reference_squares), "expert"
    )
    policy_scale = lax.rsqrt(policy_squares / D + EPSILON)[:, None]
    reference_scale = lax.rsqrt(reference_squares / D + EPSILON)[:, None]
    policy_logits = policy_partial * policy_scale
    reference_logits = reference_partial * reference_scale
    policy_rows = (policy_hidden.astype(jnp.float32) * policy_norm_gain * policy_scale).astype(
        jnp.bfloat16
    )
    reference_rows = (
        reference_hidden.astype(jnp.float32) * reference_norm_gain * reference_scale
    ).astype(jnp.bfloat16)
    live_mask = (
        (jnp.arange(SEG, dtype=jnp.int32)[None, :] < lengths[:, None])
        .reshape(-1)
        .astype(jnp.float32)
    )
    flat_ids = expert_ids.reshape(-1)
    onehot = (flat_ids[:, None] == jnp.arange(expert_count, dtype=jnp.int32)[None, :]).astype(
        jnp.int32
    )
    before = jnp.cumsum(onehot, axis=0) - onehot
    target = flat_ids * slot_count + jnp.sum(before * onehot, axis=1)
    slot_index = jnp.arange(expert_count * slot_count, dtype=jnp.int32)
    select = jnp.any(
        slot_index[:, None, None] == target.reshape(token_count, route_count)[None, :, :], axis=2
    ).astype(jnp.bfloat16)

    def pair_gates(logits):
        matches = expert_ids[:, :, None] == jnp.arange(expert_count, dtype=jnp.int32)[None, None, :]
        chosen = jnp.sum(jnp.where(matches, logits[:, None, :], 0.0), axis=2)
        return jax.nn.softmax(chosen, axis=1)

    def combine(expert_output, gates):
        picked = jnp.take(
            expert_output.reshape(expert_count * slot_count, feature_block), target, axis=0
        )
        picked = picked.reshape(token_count, route_count, feature_block).astype(jnp.float32)
        mixed_rows = jnp.sum(picked * gates[:, :, None], axis=1) * live_mask[:, None]
        return mixed_rows.astype(jnp.bfloat16)

    policy_gate_full, policy_up_full, reference_gate_full, reference_up_full = sent_together(
        (policy_gate, policy_up, reference_gate, reference_up), DP, 2, 1, 0
    )
    stacked_rows = jnp.concatenate((policy_rows, reference_rows), axis=1)
    placed = jnp.dot(select, stacked_rows, preferred_element_type=jnp.float32).astype(jnp.bfloat16)
    expert_output = mixture(
        placed.reshape(expert_count, slot_count, 2, feature_block),
        (
            (policy_gate_full[0], policy_up_full[0], policy_down[0]),
            (reference_gate_full[0], reference_up_full[0], reference_down[0]),
        ),
    )
    policy_output = expert_output[:, :, 0, :]
    reference_output = expert_output[:, :, 1, :]
    policy_mixture = combine(policy_output, pair_gates(policy_logits))
    reference_mixture = combine(reference_output, pair_gates(reference_logits))
    policy_logprob = jax.nn.log_softmax(policy_logits, axis=1)
    reference_logprob = jax.nn.log_softmax(reference_logits, axis=1)
    policy_prob = jnp.exp(policy_logprob)
    token_kl = jnp.sum(policy_prob * (policy_logprob - reference_logprob), axis=1) * live_mask
    route_onehot = onehot.reshape(token_count, route_count, expert_count)
    counts = jnp.sum(jnp.sum(route_onehot, axis=1).astype(jnp.float32) * live_mask[:, None], axis=0)
    probsum = jnp.sum(policy_prob * live_mask[:, None], axis=0)
    counts, probsum, kl_total = together((counts, probsum, jnp.sum(token_kl)), DP)
    balance = expert_count * jnp.sum(counts / (route_count * token_total) * probsum / token_total)
    loss = KL_WEIGHT * kl_total / token_total + BALANCE_WEIGHT * balance
    return (policy_mixture, reference_mixture, token_kl, loss)


def solution(mesh):
    split = Mesh(
        mesh.devices.reshape(4, 2, 2, mesh.shape["expert"]), ("dp_0", "dp_1", "dp_2", "expert")
    )
    placed = (
        P(DP, "expert"),
        P(DP, "expert"),
        P("expert"),
        P("expert"),
        P("expert", None),
        P("expert", None),
        P("expert", DP, None),
        P("expert", DP, None),
        P("expert", DP, None),
        P("expert", DP, None),
        P("expert", DP, None),
        P("expert", DP, None),
        P(DP, None),
        P(DP),
    )
    return jax.shard_map(
        per_device,
        mesh=split,
        in_specs=placed,
        out_specs=(P(DP, "expert"), P(DP, "expert"), P(DP), P()),
        check_vma=False,
    )
```

profile of v0, /device:TPU:0, one launch (start us, length us, event | category | flops | bytes accessed | tf_op | source)
XLA Modules:
  0.0 597.5 jit_solution(1766082048404732861)
XLA Ops:
  11.7 5.7 all-to-all-start
  20.5 3.3 all-to-all-done
  27.0 14.5 %all_to_all.60 = bf16[8,48,2,512]{3,1,2,0:T(8,128)(2,1)S(1)} all-to-all(bf16[8,48,2,512]{3,1,2,0:T(8,128)(2,1)S(1)} %copy.135), channel_id=1, replica_groups=mesh['dp_0'=4,'dp_1'=2,'dp_2'=2,'expert'=8] {'expert'}, dimensions={0} | all-to-all | bytes 1572864 | tf_op jit(solution)/shard_map/all_to_all | solution.py:76
  43.2 18.0 %copy.140 = bf16[1,256,8192]{1,0,2:T(2,128)(2,1)} copy(bf16[1,256,8192]{2,1,0:T(8,128)(2,1)} %param.27) | data formatting | bytes 8388608 | tf_op args[10]
  61.2 17.9 %copy.139 = bf16[1,256,8192]{1,0,2:T(2,128)(2,1)} copy(bf16[1,256,8192]{2,1,0:T(8,128)(2,1)} %param.26) | data formatting | bytes 8388608 | tf_op args[9]
  79.1 17.9 %copy.138 = bf16[1,256,8192]{1,0,2:T(2,128)(2,1)} copy(bf16[1,256,8192]{2,1,0:T(8,128)(2,1)} %param.24) | data formatting | bytes 8388608 | tf_op args[7]
  97.0 17.9 %copy.137 = bf16[1,256,8192]{1,0,2:T(2,128)(2,1)} copy(bf16[1,256,8192]{2,1,0:T(8,128)(2,1)} %param.23) | data formatting | bytes 8388608 | tf_op args[6]
  114.9 41.9 %pad_maximum_fusion = bf16[4,256,8192]{1,0,2:T(4,128)(2,1)} fusion(bf16[1,256,8192]{1,0,2:T(2,128)(2,1)} %copy.140, bf16[1,256,8192]{1,0,2:T(2,128)(2,1)} %copy.139, bf16[1,256,8192]{1,0,2:T(2,128)(2,1)} %copy.138, bf16[1,256,8192]{1,0,2:T(2,128)(2,1)} %copy.137), kind=kLoop, calls=%fused_computation.2 | loop fusion | flops 67108864 | bytes 33554432 | tf_op jit(solution)/shard_map/concatenate | solution.py:50
  156.8 194.3 %all_to_all.61 = bf16[4,256,8192]{1,0,2:T(4,128)(2,1)S(1)} all-to-all(bf16[4,256,8192]{1,0,2:T(4,128)(2,1)} %pad_maximum_fusion), channel_id=1, replica_groups=mesh['dp_0'=4,'dp_1'=2,'dp_2'=2,'expert'=8] {'dp_0','dp_1','dp_2'}, dimensions={2} | all-to-all | bytes 33554432 | tf_op jit(solution)/shard_map/all_to_all | solution.py:51
  351.1 11.6 %copy.141 = bf16[4,256,8192]{1,2,0:T(8,128)(2,1)S(1)} copy(bf16[4,256,8192]{1,0,2:T(4,128)(2,1)S(1)} %all_to_all.61) | data formatting | bytes 33554432 | tf_op jit(solution)/shard_map/all_to_all | solution.py:51
  362.7 5.9 fusion.39
  368.6 6.4 %copy.144 = bf16[1,16,256,512]{3,2,1,0:T(8,128)(2,1)} copy(bf16[1,16,256,512]{2,3,1,0:T(8,128)(2,1)} %get-tuple-element.21) | data formatting | bytes 8388608 | tf_op jit(solution)/shard_map/split | solution.py:52
  375.0 6.4 %copy.145 = bf16[1,16,256,512]{3,2,1,0:T(8,128)(2,1)} copy(bf16[1,16,256,512]{2,3,1,0:T(8,128)(2,1)} %get-tuple-element.20) | data formatting | bytes 8388608 | tf_op jit(solution)/shard_map/split | solution.py:52
  381.4 6.4 %copy.142 = bf16[1,16,256,512]{3,2,1,0:T(8,128)(2,1)} copy(bf16[1,16,256,512]{2,3,1,0:T(8,128)(2,1)} %get-tuple-element.22) | data formatting | bytes 8388608 | tf_op jit(solution)/shard_map/split | solution.py:52
  387.8 6.4 %copy.143 = bf16[1,16,256,512]{3,2,1,0:T(8,128)(2,1)} copy(bf16[1,16,256,512]{2,3,1,0:T(8,128)(2,1)} %get-tuple-element.19) | data formatting | bytes 8388608 | tf_op jit(solution)/shard_map/split | solution.py:52
  394.2 6.9 %fusion.5 = f32[768,512]{1,0:T(8,128)S(1)} fusion(bf16[4096,512]{1,0:T(8,128)(2,1)} %bitcast.85, bf16[768,2,4096]{2,0,1:T(8,128)(2,1)} %all-gather.2.cloned.1.call-done), kind=kOutput, calls=%fused_computation.13 | convolution fusion | flops 3221225472 | bytes 12058624 | tf_op jit(solution)/shard_map/dot_general | solution.py:66
  401.1 2.0 copy-done.6
  403.1 3.6 multiply_convert_fusion
  406.7 3.6 fusion.1
  410.4 3.4 fusion.3
  413.8 3.6 multiply_convert_fusion.1
  417.4 6.0 %fusion = bf16[8,2,48,1,4096]{4,2,1,0,3:T(8,128)(2,1)S(1)} fusion(bf16[8,2,48,512]{3,2,1,0:T(8,128)(2,1)S(1)} %bitcast.90, bf16[1,512,4096]{2,1,0:T(8,128)(2,1)} %param.25), kind=kOutput, calls=%fused_computation.8 | convolution fusion | flops 3224371200 | bytes 11272192 | tf_op jit(solution)/shard_map/dot_general | solution.py:69
  424.7 5.2 copy.146
  429.9 21.0 %reduce-scatter.3.cloned.1.call-done = bf16[8,48,2,4096]{3,1,2,0:T(8,128)(2,1)} async-done(((bf16[16,48,2,4096]{3,1,2,0:T(8,128)(2,1)}), bf16[8,48,2,4096]{3,1,2,0:T(8,128)(2,1)}) %reduce-scatter.3.cloned.1.call-update) | async-done | bytes 6291472 | tf_op jit(solution)/shard_map/reduce_scatter | solution.py:27
  454.3 7.1 %all-to-all-start.4 = ((f32[16,1,17]{2,1,0:T(1,128)}), f32[16,1,17]{2,1,0:T(1,128)S(1)}, u32[]{:S(2)}, u32[]{:S(2)}) async-start(f32[16,1,17]{2,1,0:T(1,128)} %broadcast_in_dim.35), calls=%async_computation.6 | async-start | bytes 16384 | tf_op jit(solution)/shard_map/all_to_all | solution.py:33
  461.4 94.0 %reduce-scatter.5.cloned.1.call-done = bf16[1,48,2,4096]{3,1,2,0:T(8,128)(2,1)} async-done(((bf16[8,48,2,4096]{3,1,2,0:T(8,128)(2,1)}), bf16[1,48,2,4096]{3,1,2,0:T(8,128)(2,1)}) %reduce-scatter.5.cloned.1.call-update) | async-done | bytes 786448 | tf_op jit(solution)/shard_map/reduce_scatter | solution.py:28
  555.4 4.9 copy.147
  560.4 4.0 reshape.301
  564.3 4.3 all-to-all-start.3
  571.6 9.3 %all-to-all-done.3 = bf16[8,2,24576]{2,1,0:T(2,128)(2,1)S(1)} async-done(((bf16[8,2,24576]{2,1,0:T(2,128)(2,1)}), bf16[8,2,24576]{2,1,0:T(2,128)(2,1)S(1)}, u32[]{:S(2)}, u32[]{:S(2)}) %all-to-all-start.3) | async-done | bytes 786464 | tf_op jit(solution)/shard_map/all_to_all | solution.py:86
  580.8 2.1 reshape.302
  582.9 1.3 copy.160
  (99 shorter events, 24.1 us)
Async XLA Ops:
  7.2 1.1 copy-start
  11.7 12.1 %all-to-all-start = ((f32[8,1,2304]{2,1,0:T(1,128)}), f32[8,1,2304]{2,1,0:T(1,128)S(1)}, u32[]{:S(2)}, u32[]{:S(2)}) async-start(f32[8,1,2304]{2,1,0:T(1,128)} %broadcast_in_dim.31), calls=%async_computation | async-start | bytes 147456 | tf_op jit(solution)/shard_map/all_to_all | solution.py:33
  17.4 376.8 %all-gather.2.cloned.1.call-start = ((), (), s32[]{:S(2)}) async-start(), calls=%async_computation.7 | async-start | bytes 13369344 | tf_op jit(solution)/shard_map/all_gather | solution.py:79
  43.2 407.8 %reduce-scatter.3.cloned.1.call-start = ((), (), s32[]{:S(2)}) async-start(), calls=%async_computation.8 | async-start | bytes 18874368 | tf_op jit(solution)/shard_map/reduce_scatter | solution.py:27
  394.2 6.9 %copy-start.4 = (bf16[1,16,256,512]{3,2,1,0:T(8,128)(2,1)S(1)}, bf16[1,16,256,512]{3,2,1,0:T(8,128)(2,1)}, u32[]{:S(2)}) copy-start(bf16[1,16,256,512]{3,2,1,0:T(8,128)(2,1)} %copy.145) | copy-start | bytes 12582916
  394.2 8.9 %copy-start.6 = (bf16[768,2,4096]{2,0,1:T(8,128)(2,1)S(1)}, bf16[768,2,4096]{2,0,1:T(8,128)(2,1)}, u32[]{:S(2)}) copy-start(bf16[768,2,4096]{2,0,1:T(8,128)(2,1)} %all-gather.2.cloned.1.call-done) | copy-start | bytes 37748740
  403.1 3.6 copy-start.7
  406.7 3.7 copy-start.2
  410.4 3.4 copy-start.3
  429.9 21.1 %copy-start.8 = (s32[4]{0:T(128)S(1)}, s32[4]{0:T(128)}, u32[]{:S(2)}) copy-start(s32[4]{0:T(128)} %param.30) | copy-start | bytes 52
  429.9 21.3 %copy-start.5 = (s32[128,2]{0,1:T(2,128)S(1)}, s32[128,2]{0,1:T(2,128)}, u32[]{:S(2)}) copy-start(s32[128,2]{0,1:T(2,128)} %param.29) | copy-start | bytes 3076
  429.9 125.5 %reduce-scatter.5.cloned.1.call-start = ((), (), s32[]{:S(2)}) async-start(), calls=%async_computation.9 | async-start | bytes 7077888 | tf_op jit(solution)/shard_map/reduce_scatter | solution.py:28
  454.3 110.0 %all-to-all-start.4 = ((f32[16,1,17]{2,1,0:T(1,128)}), f32[16,1,17]{2,1,0:T(1,128)S(1)}, u32[]{:S(2)}, u32[]{:S(2)}) async-start(f32[16,1,17]{2,1,0:T(1,128)} %broadcast_in_dim.35), calls=%async_computation.6 | async-start | bytes 16384 | tf_op jit(solution)/shard_map/all_to_all | solution.py:33
  564.3 16.5 %all-to-all-start.3 = ((bf16[8,2,24576]{2,1,0:T(2,128)(2,1)}), bf16[8,2,24576]{2,1,0:T(2,128)(2,1)S(1)}, u32[]{:S(2)}, u32[]{:S(2)}) async-start(bf16[8,2,24576]{2,1,0:T(2,128)(2,1)} %reshape.301), calls=%async_computation.5 | async-start | bytes 1572864 | tf_op jit(solution)/shard_map/all_to_all | solution.py:86
  585.7 4.1 copy-start.1
Sparse Core Ops, SparseCore 0:
  43.3 91.0 all-gather.1
  430.0 20.9 reduce-scatter.2
  454.9 100.4 reduce-scatter.4
where the time goes:
time: 601 us; the launch traced here: 598 us
  blocking collectives  209 us (35%)
  local copies, waits for them, and re-layouts  144 us (24%)
  waiting for transfers between devices  128 us (21%)
  other arithmetic  53.1 us (9%)
  matrix products  30 us (5%)
  starting transfers between devices  17.3 us (3%)
  between operations  16.6 us (3%)
    all_to_all x1, blocking collectives, sent_together(): lax.all_to_all(both, axis, split_axis=split_dim, concat_axis=concat_dim,...  194 us
    reduce_scatter x1, waiting for transfers between devices, sum_by_chip(): return lax.psum_scatter(tiles, chips, scatter_dimension=0, tiled=True)[0]  94 us
    unnamed x25, local copies, waits for them, and re-layouts  80.6 us
    concatenate x1, other arithmetic, sent_together(): both = jnp.concatenate(arrays, axis=along)  41.9 us
    split x5, local copies, waits for them, and re-layouts, sent_together(): jnp.split(whole, [sum(widths[:k]) for k in range(1, len(widths))], axis=a...  31.5 us
    reduce_scatter x1, waiting for transfers between devices, sum_by_chip(): tiles = lax.psum_scatter(tiles, core, scatter_dimension=0, tiled=True)  21 us
    all_to_all x1, blocking collectives, mixture(): lax.all_to_all(slot_rows, 'expert', split_axis=0, concat_axis=3, tiled=True)  14.5 us
    all_to_all x2, starting transfers between devices, from_everyone(): return lax.all_to_all(copies, axis, split_axis=0, concat_axis=0, tiled=True)  12.8 us
  transfers between devices with their start and end apart: 6, of which 4 were waited for; matrix products, arithmetic and copies ran while one was open for 29% of the time, Pallas kernels for 0%

commit v1 on v0

v1 whole, which is shorter than its diff:
```python
import jax
import jax.numpy as jnp
from jax import lax
from jax.experimental import pallas as pl
from jax.sharding import Mesh
from jax.sharding import PartitionSpec as P

D = 4096
SEG = 32
ROW = "dp_y"
COLUMN = "dp_z"
CORE = "dp_core"
DP = (ROW, COLUMN, CORE)


EPSILON = 1e-05
KL_WEIGHT = 1.0
BALANCE_WEIGHT = 0.5
PACK = 4


def pack_kernel(gate_ref, up_ref, *packed_refs):
    parts = len(packed_refs)
    width = gate_ref.shape[1] // (PACK * parts)
    for k in range(PACK):
        for part, packed_ref in enumerate(packed_refs):
            taken = slice((k * parts + part) * width, (k * parts + part + 1) * width)
            packed_ref[k, :, :width] = gate_ref[:, taken]
            packed_ref[k, :, width:] = up_ref[:, taken]


def packed(gate, up, peers, parts):
    rows, width = gate.shape[1:]
    piece = width // peers
    taken = pl.BlockSpec((None, rows, PACK * piece), lambda j: (0, 0, j))
    return pl.pallas_call(
        pack_kernel,
        grid=(peers // PACK,),
        in_specs=[taken, taken],
        out_specs=[pl.BlockSpec((PACK, rows, 2 * piece // parts), lambda j: (j, 0, 0))] * parts,
        out_shape=[jax.ShapeDtypeStruct((peers, rows, 2 * piece // parts), gate.dtype)] * parts,
        cost_estimate=pl.CostEstimate(
            flops=0, bytes_accessed=8 * rows * width, transcendentals=0
        ),
    )(gate, up)


def router_terms(hidden, norm_gain, router):
    values = hidden.astype(jnp.float32)
    partial_logits = jnp.dot(values * norm_gain, router, precision=lax.Precision.HIGHEST)
    return (partial_logits, jnp.sum(values * values, axis=1))


def exchange(value, axis):
    return lax.all_to_all(value, axis, split_axis=0, concat_axis=0, tiled=True)


def from_xor(value, axis, step):
    return lax.ppermute(value, axis, [(i, i ^ step) for i in range(lax.axis_size(axis))])


def from_ahead(value, axis, step):
    size = lax.axis_size(axis)
    return lax.ppermute(value, axis, [((i + step) % size, i) for i in range(size)])


def of_everyone(value, *axes):
    for axis in axes:
        step = 1
        while step < lax.axis_size(axis):
            value = value + from_xor(value, axis, step)
            step *= 2
    return value


def chip_pair(own):
    return jnp.stack((own, from_xor(own, COLUMN, 1)))


def all_chips(pair):
    ahead, behind = from_ahead(pair, ROW, 1), from_ahead(pair, ROW, 3)
    return (pair, ahead, from_ahead(pair, ROW, 2), behind)


def gathered(chips):
    pieces = (*chips, *(from_xor(chip, CORE, 1) for chip in chips))
    models, slot_count, width = chips[0].shape[1:]
    return [
        jnp.concatenate([piece[:, m].reshape(-1, width) for piece in pieces])
        for m in range(models)
    ]


def split_in_three(values):
    rows = []
    for _ in range(3):
        rows.append(values.astype(jnp.bfloat16))
        values = values - rows[-1].astype(jnp.float32)
    return jnp.stack(rows)


def normed_rows(arrived, gain):
    values = arrived.astype(jnp.float32)
    scale = lax.rsqrt(jnp.sum(values * values, axis=(0, 2)) / D + EPSILON)
    normed = (values * gain[:, None, :] * scale[None, :, None]).astype(jnp.bfloat16)
    return normed.transpose(1, 0, 2).reshape(arrived.shape[1], -1)


def hidden_units(rows, gate_up):
    both = jnp.dot(rows, gate_up, preferred_element_type=jnp.float32)
    width = both.shape[1] // 2
    return (jax.nn.silu(both[:, :width]) * both[:, width:]).astype(jnp.bfloat16)


def added(*terms):
    total = terms[0].astype(jnp.float32)
    for term in terms[1:]:
        total = total + term.astype(jnp.float32)
    return total.astype(jnp.bfloat16)


def chip_terms(hidden, down):
    half = hidden.shape[0] // 2

    def part(rows):
        return jnp.dot(rows, down, preferred_element_type=jnp.float32)

    arrived = from_xor(part(hidden[half:]).astype(jnp.bfloat16), CORE, 1)
    return added(part(hidden[:half]), arrived).reshape(lax.axis_size(ROW), -1, down.shape[1])


def toward_neighbours(chip):
    middle = chip.shape[2] // 2
    left, right = chip[2, :, :middle], chip[2, :, middle:]
    ahead = jnp.concatenate(
        (added(chip[1, :, :middle], from_ahead(left, ROW, 3)), chip[1, :, middle:]), axis=1
    )
    behind = jnp.concatenate(
        (chip[3, :, :middle], added(chip[3, :, middle:], from_ahead(right, ROW, 1))), axis=1
    )
    return (ahead, behind)


def row_terms(own, ahead, behind):
    return added(own, from_ahead(ahead, ROW, 3), from_ahead(behind, ROW, 1))


def column_terms(row):
    half = row.shape[0] // 2
    return added(row[:half], from_xor(row[half:], COLUMN, 1))


def per_device(
    policy_hidden,
    reference_hidden,
    policy_norm_gain,
    reference_norm_gain,
    policy_router,
    reference_router,
    policy_gate,
    policy_up,
    policy_down,
    reference_gate,
    reference_up,
    reference_down,
    expert_ids,
    lengths,
):
    expert_count = lax.axis_size("expert")
    peers = lax.axis_size(DP)
    token_count, feature_block = policy_hidden.shape
    route_count = expert_ids.shape[1]
    slot_count = 3 * token_count // expert_count
    token_total = float(token_count * peers)

    policy_partial, policy_squares = router_terms(policy_hidden, policy_norm_gain, policy_router)
    reference_partial, reference_squares = router_terms(
        reference_hidden, reference_norm_gain, reference_router
    )
    sums = of_everyone(
        jnp.concatenate(
            (policy_partial.T, reference_partial.T, policy_squares[None], reference_squares[None])
        ),
        "expert",
    ).T
    policy_scale = lax.rsqrt(sums[:, 2 * expert_count] / D + EPSILON)[:, None]
    reference_scale = lax.rsqrt(sums[:, 2 * expert_count + 1] / D + EPSILON)[:, None]
    policy_logits = sums[:, :expert_count] * policy_scale
    reference_logits = sums[:, expert_count : 2 * expert_count] * reference_scale
    flat_ids = expert_ids.reshape(-1)
    onehot = (flat_ids[:, None] == jnp.arange(expert_count, dtype=jnp.int32)[None, :]).astype(
        jnp.int32
    )
    before = jnp.cumsum(onehot, axis=0) - onehot
    within = jnp.sum(before * onehot, axis=1)
    slot_index = jnp.arange(expert_count * slot_count, dtype=jnp.int32)
    target = (flat_ids * slot_count + within).reshape(token_count, route_count)
    select = jnp.any(slot_index[:, None, None] == target[None, :, :], axis=2)
    placed = jnp.dot(
        select.astype(jnp.bfloat16),
        jnp.concatenate((policy_hidden, reference_hidden), axis=1),
        preferred_element_type=jnp.float32,
    ).astype(jnp.bfloat16)
    gain_rows = split_in_three(jnp.concatenate((policy_norm_gain, reference_norm_gain)))
    gain_rows = jnp.pad(gain_rows, ((0, 13), (0, 0)))
    arrived = exchange(
        jnp.concatenate(
            (
                placed.reshape(expert_count, slot_count, 2 * feature_block),
                jnp.broadcast_to(gain_rows, (expert_count, *gain_rows.shape)),
            ),
            axis=1,
        ),
        "expert",
    )
    gains = jnp.sum(arrived[:, slot_count : slot_count + 3].astype(jnp.float32), axis=1)
    arrived = arrived[:, :slot_count]
    live_mask = (
        (jnp.arange(SEG, dtype=jnp.int32)[None, :] < lengths[:, None])
        .reshape(-1)
        .astype(jnp.float32)
    )
    chosen_slot = target[:, :, None] == slot_index[None, None, :]

    def slot_weights(logits):
        matches = expert_ids[:, :, None] == jnp.arange(expert_count, dtype=jnp.int32)[None, None, :]
        chosen = jnp.sum(jnp.where(matches, logits[:, None, :], 0.0), axis=2)
        gates = jax.nn.softmax(chosen, axis=1) * live_mask[:, None]
        return jnp.sum(jnp.where(chosen_slot, gates[:, :, None], 0.0), axis=1)

    policy_weights = slot_weights(policy_logits)
    reference_weights = slot_weights(reference_logits)
    policy_logprob = jax.nn.log_softmax(policy_logits, axis=1)
    reference_logprob = jax.nn.log_softmax(reference_logits, axis=1)
    policy_prob = jnp.exp(policy_logprob)
    token_kl = jnp.sum(policy_prob * (policy_logprob - reference_logprob), axis=1) * live_mask
    route_onehot = onehot.reshape(token_count, route_count, expert_count)
    counts = jnp.sum(jnp.sum(route_onehot, axis=1).astype(jnp.float32) * live_mask[:, None], axis=0)
    probsum = jnp.sum(policy_prob * live_mask[:, None], axis=0)
    local_totals = jnp.concatenate((counts, probsum, jnp.sum(token_kl)[None]))

    own = jnp.stack(
        (
            normed_rows(arrived[:, :, :feature_block], gains[:, :feature_block]),
            normed_rows(arrived[:, :, feature_block:], gains[:, feature_block:]),
        )
    )
    (policy_packed,) = packed(policy_gate, policy_up, peers, 1)
    first_packed, second_packed = packed(reference_gate, reference_up, peers, 2)
    policy_gate_up = exchange(policy_packed, DP).reshape(D, -1)
    totals = local_totals + from_xor(local_totals, ROW, 1)
    pair, totals, policy_weights, reference_weights, policy_gate_up, first_packed, second_packed = (
        lax.optimization_barrier(
            (
                chip_pair(own),
                totals,
                policy_weights,
                reference_weights,
                policy_gate_up,
                first_packed,
                second_packed,
            )
        )
    )

    first_gate_up = exchange(first_packed, DP).reshape(D, -1)
    policy_rows, reference_rows = gathered(all_chips(pair))
    policy_chip = chip_terms(hidden_units(policy_rows, policy_gate_up), policy_down[0])
    totals = totals + from_xor(totals, ROW, 2)
    policy_chip, totals, first_gate_up, second_packed = lax.optimization_barrier(
        (policy_chip, totals, first_gate_up, second_packed)
    )

    second_gate_up = exchange(second_packed, DP).reshape(D, -1)
    first_hidden = hidden_units(reference_rows, first_gate_up)
    policy_row = row_terms(policy_chip[0], *toward_neighbours(policy_chip))
    totals = totals + from_xor(totals, COLUMN, 1)
    first_hidden, policy_row, totals, second_gate_up = lax.optimization_barrier(
        (first_hidden, policy_row, totals, second_gate_up)
    )

    second_hidden = hidden_units(reference_rows, second_gate_up)
    reference_chip = chip_terms(
        jnp.concatenate((first_hidden, second_hidden), axis=1), reference_down[0]
    )
    policy_output = column_terms(policy_row)
    reference_row = row_terms(reference_chip[0], *toward_neighbours(reference_chip))
    reference_output = column_terms(reference_row)
    totals = totals + from_xor(totals, CORE, 1)
    counts, probsum = totals[:expert_count], totals[expert_count : 2 * expert_count]
    kl_total = totals[2 * expert_count]
    balance = expert_count * jnp.sum(counts / (route_count * token_total) * probsum / token_total)
    loss = KL_WEIGHT * kl_total / token_total + BALANCE_WEIGHT * balance
    outputs = jnp.stack((policy_output, reference_output), axis=1)
    outputs = outputs.reshape(slot_count, 2, expert_count, feature_block).transpose(2, 0, 1, 3)
    outputs = exchange(outputs.reshape(expert_count, slot_count, -1), "expert")
    outputs = outputs.reshape(expert_count * slot_count, -1)

    def mixture(weights, output):
        mixed = jnp.dot(weights, output.astype(jnp.float32), precision=lax.Precision.HIGHEST)
        return mixed.astype(jnp.bfloat16)

    policy_mixture = mixture(policy_weights, outputs[:, :feature_block])
    reference_mixture = mixture(reference_weights, outputs[:, feature_block:])
    return (policy_mixture, reference_mixture, token_kl, loss)


def solution(mesh):
    split = Mesh(mesh.devices.reshape(4, 2, 2, mesh.shape["expert"]), (*DP, "expert"))
    placed = (
        P(DP, "expert"),
        P(DP, "expert"),
        P("expert"),
        P("expert"),
        P("expert", None),
        P("expert", None),
        P("expert", DP, None),
        P("expert", DP, None),
        P("expert", DP, None),
        P("expert", DP, None),
        P("expert", DP, None),
        P("expert", DP, None),
        P(DP, None),
        P(DP),
    )
    return jax.shard_map(
        per_device,
        mesh=split,
        in_specs=placed,
        out_specs=(P(DP, "expert"), P(DP, "expert"), P(DP), P()),
        check_vma=False,
    )
```

time: 601 us -> 460 us (0.77)
  blocking collectives: 209 us -> 0 us
  waiting for transfers between devices: 128 us -> 259 us
  local copies, waits for them, and re-layouts: 144 us -> 27 us
  starting transfers between devices: 17.3 us -> 105 us
  other arithmetic: 53.1 us -> 14.7 us
  Pallas kernels: 0 us -> 14.1 us
  between operations: 16.6 us -> 3.83 us
    ppermute x0 -> x27, waiting for transfers between devices: none -> 228 us  [the longest x11 119 us: from_ahead(): lax.ppermute(value, axis, [((i + step) % size, i) for i in range(size)])]
    all_to_all x2 -> x0, blocking collectives: 209 us -> none  [the longest x1 194 us: sent_together(): lax.all_to_all(both, axis, split_axis=split_dim, concat_axis=concat_dim,...]
    reduce_scatter x2 -> x0, waiting for transfers between devices: 115 us -> none  [the longest x1 94 us: sum_by_chip(): return lax.psum_scatter(tiles, chips, scatter_dimension=0, tiled=True)[0]]
    ppermute x0 -> x27, starting transfers between devices: none -> 75 us  [the longest x16 49 us: from_xor(): lax.ppermute(value, axis, [(i, i ^ step) for i in range(lax.axis_size(axi...]
    unnamed x25 -> x52, local copies, waits for them, and re-layouts: 80.6 us -> 10.8 us
    concatenate x3 -> x7, other arithmetic: 42.6 us -> 2.06 us  [the longest x1 1.06 us: per_device(): jnp.concatenate((placed.reshape(expert_count, slot_count, 2 * feature_blo...]
    split x5 -> x0, local copies, waits for them, and re-layouts: 31.5 us -> none  [sent_together(): jnp.split(whole, [sum(widths[:k]) for k in range(1, len(widths))], axis=a...]
    all_to_all x3 -> x5, waiting for transfers between devices: 12.6 us -> 30.7 us  [exchange(): return lax.all_to_all(value, axis, split_axis=0, concat_axis=0, tiled=True)]
  transfers between devices with their start and end apart: 6 -> 32, of which waited for: 4 -> 20; matrix products, arithmetic and copies ran while one was open for 29% -> 11% of each run, Pallas kernels for 0% -> 3%
where the time goes in v1:
time: 460 us; the launch traced here: 459 us
  waiting for transfers between devices  259 us (56%)
  starting transfers between devices  105 us (23%)
  matrix products  36 us (8%)
  local copies, waits for them, and re-layouts  27 us (6%)
  other arithmetic  14.7 us (3%)
  Pallas kernels  14.1 us (3%)
    ppermute x11, waiting for transfers between devices, from_ahead(): lax.ppermute(value, axis, [((i + step) % size, i) for i in range(size)])  119 us
    ppermute x16, waiting for transfers between devices, from_xor(): lax.ppermute(value, axis, [(i, i ^ step) for i in range(lax.axis_size(axi...  109 us
    ppermute x16, starting transfers between devices, from_xor(): lax.ppermute(value, axis, [(i, i ^ step) for i in range(lax.axis_size(axi...  49 us
    all_to_all x5, waiting for transfers between devices, exchange(): return lax.all_to_all(value, axis, split_axis=0, concat_axis=0, tiled=True)  30.7 us
    all_to_all x5, starting transfers between devices, exchange(): return lax.all_to_all(value, axis, split_axis=0, concat_axis=0, tiled=True)  30 us
    ppermute x11, starting transfers between devices, from_ahead(): lax.ppermute(value, axis, [((i + step) % size, i) for i in range(size)])  26.1 us
    dot_general x3, matrix products, hidden_units(): both = jnp.dot(rows, gate_up, preferred_element_type=jnp.float32)  24.7 us
    pallas_call x2, Pallas kernels, packed(): pl.pallas_call(pack_kernel, grid=(peers // PACK,), in_specs=[taken, taken...  14.1 us
  transfers between devices with their start and end apart: 32, of which 20 were waited for; matrix products, arithmetic and copies ran while one was open for 11% of the time, Pallas kernels for 3%

profile of v1, /device:TPU:0, one launch (start us, length us, event | category | flops | bytes accessed | tf_op | source)
XLA Modules:
  0.0 459.4 jit_solution(12477685643259562606)
XLA Ops:
  7.5 5.7 %all-to-all-start = ((bf16[8,64,1024]{2,1,0:T(8,128)(2,1)}), bf16[8,64,1024]{2,1,0:T(8,128)(2,1)S(1)}, u32[]{:S(2)}, u32[]{:S(2)}) async-start(bf16[8,64,1024]{2,1,0:T(8,128)(2,1)} %pad_maximum_fusion.1), calls=%async_computation | async-start | bytes 2097152 | tf_op jit(solution)/shard_map/all_to_all | solution.py:55
  13.2 7.0 %shard_map.165 = bf16[16,256,1024]{2,1,0:T(8,128)(2,1)} custom-call(bf16[1,256,8192]{2,1,0:T(8,128)(2,1)} %gate_ref.2, bf16[1,256,8192]{2,1,0:T(8,128)(2,1)} %up_ref.2), custom_call_target="tpu_custom_call" | custom-call | bytes 16777216 | tf_op jit(solution)/shard_map/pallas_call | solution.py:36
  20.3 8.6 %all-to-all-done = bf16[8,64,1024]{2,1,0:T(8,128)(2,1)S(1)} async-done(((bf16[8,64,1024]{2,1,0:T(8,128)(2,1)}), bf16[8,64,1024]{2,1,0:T(8,128)(2,1)S(1)}, u32[]{:S(2)}, u32[]{:S(2)}) %all-to-all-start) | async-done | bytes 1048608 | tf_op jit(solution)/shard_map/all_to_all | solution.py:55
  28.9 7.6 %all-to-all-start.1 = ((bf16[16,256,1024]{2,1,0:T(8,128)(2,1)}), bf16[16,256,1024]{2,1,0:T(8,128)(2,1)}, u32[]{:S(2)}, u32[]{:S(2)}) async-start(bf16[16,256,1024]{2,1,0:T(8,128)(2,1)} %shard_map.165), calls=%async_computation.1 | async-start | bytes 16777216 | tf_op jit(solution)/shard_map/all_to_all | solution.py:55
  38.5 2.8 collective-permute-done.1
  42.3 4.3 collective-permute-done.2
  46.7 7.1 %shard_map.166 = (bf16[16,256,512]{2,1,0:T(8,128)(2,1)}, bf16[16,256,512]{2,1,0:T(8,128)(2,1)}) custom-call(bf16[1,256,8192]{2,1,0:T(8,128)(2,1)} %gate_ref.3, bf16[1,256,8192]{2,1,0:T(8,128)(2,1)} %up_ref.3), custom_call_target="tpu_custom_call" | custom-call | bytes 16777216 | tf_op jit(solution)/shard_map/pallas_call | solution.py:36
  53.8 18.1 %collective-permute-done.3 = f32[18,128]{1,0:T(8,128)S(1)} collective-permute-done((f32[18,128]{1,0:T(8,128)S(1)}, f32[18,128]{1,0:T(8,128)S(1)}, u32[]{:S(2)}, u32[]{:S(2)}) %collective-permute-start.3) | collective-permute-done | bytes 9248 | tf_op jit(solution)/shard_map/ppermute | solution.py:59
  74.9 26.3 %collective-permute-start = (bf16[2,48,4096]{2,1,0:T(8,128)(2,1)S(1)}, bf16[2,48,4096]{2,1,0:T(8,128)(2,1)S(1)}, u32[]{:S(2)}, u32[]{:S(2)}) collective-permute-start(bf16[2,48,4096]{2,1,0:T(8,128)(2,1)S(1)} %constant_dynamic-update-slice_fusion), channel_id=1, source_target_pairs={{0,16},{16,0},{1,17},{17,1},{2,18},{18,2},{3,19},{19,3},{4,20},{20... | collective-permute-start | bytes 2359304 | tf_op jit(solution)/shard_map/ppermute | solution.py:59
  102.0 13.9 %collective-permute-start.4 = (f32[17]{0:T(128)S(1)}, f32[17]{0:T(128)S(1)}, u32[]{:S(2)}, u32[]{:S(2)}) collective-permute-start(f32[17]{0:T(128)S(1)} %pad_maximum_fusion.10), channel_id=1, source_target_pairs={{0,32},{32,0},{64,96},{96,64},{1,33},{33,1},{65,97},{97,65},{2,34}... | collective-permute-start | bytes 212 | tf_op jit(solution)/shard_map/ppermute | solution.py:59
  116.8 52.1 %collective-permute-done.4 = f32[17]{0:T(128)S(1)} collective-permute-done((f32[17]{0:T(128)S(1)}, f32[17]{0:T(128)S(1)}, u32[]{:S(2)}, u32[]{:S(2)}) %collective-permute-start.4) | collective-permute-done | bytes 100 | tf_op jit(solution)/shard_map/ppermute | solution.py:59
  170.1 4.2 collective-permute-start.6
  177.6 5.7 %all-to-all-start.2 = ((bf16[16,256,512]{2,1,0:T(8,128)(2,1)}), bf16[16,256,512]{2,1,0:T(8,128)(2,1)}, u32[]{:S(2)}, u32[]{:S(2)}) async-start(bf16[16,256,512]{2,1,0:T(8,128)(2,1)} %get-tuple-element.28), calls=%async_computation.2 | async-start | bytes 8388608 | tf_op jit(solution)/shard_map/all_to_all | solution.py:55
  183.2 24.4 %collective-permute-done.5 = bf16[2,2,48,4096]{3,2,1,0:T(8,128)(2,1)} collective-permute-done((bf16[2,2,48,4096]{3,2,1,0:T(8,128)(2,1)S(1)}, bf16[2,2,48,4096]{3,2,1,0:T(8,128)(2,1)}, u32[]{:S(2)}, u32[]{:S(2)}) %collective-permute-start.5) | collective-permute-done | bytes 1572896 | tf_op jit(solution)/shard_map/ppermute | solution.py:64
  212.6 30.3 %collective-permute-done.7 = bf16[2,2,48,4096]{3,2,1,0:T(8,128)(2,1)} collective-permute-done((bf16[2,2,48,4096]{3,2,1,0:T(8,128)(2,1)S(1)}, bf16[2,2,48,4096]{3,2,1,0:T(8,128)(2,1)}, u32[]{:S(2)}, u32[]{:S(2)}) %collective-permute-start.7) | collective-permute-done | bytes 1572896 | tf_op jit(solution)/shard_map/ppermute | solution.py:64
  253.6 11.0 %fusion.78 = f32[768,1024]{1,0:T(8,128)S(1)} fusion(bf16[768,4096]{1,0:T(8,128)(2,1)} %constant_dynamic-update-slice_fusion.10, bf16[4096,1024]{1,0:T(8,128)(2,1)} %bitcast.17), kind=kOutput, calls=%fused_computation.179 | convolution fusion | flops 6442450944 | bytes 17825792 | tf_op jit(solution)/shard_map/dot_general | solution.py:110
  267.9 2.6 copy-done.8
  274.7 15.2 %all-to-all-done.2 = bf16[16,256,512]{2,1,0:T(8,128)(2,1)} async-done(((bf16[16,256,512]{2,1,0:T(8,128)(2,1)}), bf16[16,256,512]{2,1,0:T(8,128)(2,1)}, u32[]{:S(2)}, u32[]{:S(2)}) %all-to-all-start.2) | async-done | bytes 4194336 | tf_op jit(solution)/shard_map/all_to_all | solution.py:55
  294.1 7.3 %all-to-all-start.3 = ((bf16[16,256,512]{2,1,0:T(8,128)(2,1)}), bf16[16,256,512]{2,1,0:T(8,128)(2,1)}, u32[]{:S(2)}, u32[]{:S(2)}) async-start(bf16[16,256,512]{2,1,0:T(8,128)(2,1)} %get-tuple-element.33), calls=%async_computation.3 | async-start | bytes 8388608 | tf_op jit(solution)/shard_map/all_to_all | solution.py:55
  303.6 3.4 collective-permute-start.18
  308.5 6.8 %collective-permute-start.15 = (bf16[96,4096]{1,0:T(8,128)(2,1)S(1)}, bf16[96,4096]{1,0:T(8,128)(2,1)S(1)}, u32[]{:S(2)}, u32[]{:S(2)}) collective-permute-start(bf16[96,4096]{1,0:T(8,128)(2,1)S(1)} %pad_maximum_fusion.2), channel_id=1, source_target_pairs={{96,0},{0,32},{32,64},{64,96},{97,1},{1,33},{33,65},{65,97},{98,2}... | collective-permute-start | bytes 2359304 | tf_op jit(solution)/shard_map/ppermute | solution.py:64
  315.7 6.7 %fusion.79 = f32[768,512]{1,0:T(8,128)S(1)} fusion(bf16[768,4096]{1,0:T(8,128)(2,1)} %constant_dynamic-update-slice_fusion.2, bf16[4096,512]{1,0:T(8,128)(2,1)} %bitcast.36), kind=kOutput, calls=%fused_computation.180 | convolution fusion | flops 3221225472 | bytes 12058624 | tf_op jit(solution)/shard_map/dot_general | solution.py:110
  322.7 11.5 %collective-permute-done.18 = f32[17]{0:T(128)S(1)} collective-permute-done((f32[17]{0:T(128)S(1)}, f32[17]{0:T(128)S(1)}, u32[]{:S(2)}, u32[]{:S(2)}) %collective-permute-start.18) | collective-permute-done | bytes 100 | tf_op jit(solution)/shard_map/ppermute | solution.py:59
  334.7 36.4 %collective-permute-done.15 = bf16[96,4096]{1,0:T(8,128)(2,1)S(1)} collective-permute-done((bf16[96,4096]{1,0:T(8,128)(2,1)S(1)}, bf16[96,4096]{1,0:T(8,128)(2,1)S(1)}, u32[]{:S(2)}, u32[]{:S(2)}) %collective-permute-start.15) | collective-permute-done | bytes 786464 | tf_op jit(solution)/shard_map/ppermute | solution.py:64
  372.2 6.9 %fusion.80 = f32[768,512]{1,0:T(8,128)S(1)} fusion(bf16[768,4096]{1,0:T(8,128)(2,1)} %constant_dynamic-update-slice_fusion.2, bf16[4096,512]{1,0:T(8,128)(2,1)} %bitcast.44), kind=kOutput, calls=%fused_computation.181 | convolution fusion | flops 3221225472 | bytes 12058624 | tf_op jit(solution)/shard_map/dot_general | solution.py:110
  381.3 5.6 %collective-permute-done.20 = bf16[384,4096]{1,0:T(8,128)(2,1)S(1)} collective-permute-done((bf16[384,4096]{1,0:T(8,128)(2,1)S(1)}, bf16[384,4096]{1,0:T(8,128)(2,1)S(1)}, u32[]{:S(2)}, u32[]{:S(2)}) %collective-permute-start.20) | collective-permute-done | bytes 3145760 | tf_op jit(solution)/shard_map/ppermute | solution.py:59
  391.4 5.3 %collective-permute-start.23 = (bf16[96,2048]{1,0:T(8,128)(2,1)S(1)}, bf16[96,2048]{1,0:T(8,128)(2,1)S(1)}, u32[]{:S(2)}, u32[]{:S(2)}) collective-permute-start(bf16[96,2048]{1,0:T(8,128)(2,1)S(1)} %get-tuple-element.57), channel_id=1, source_target_pairs={{32,0},{64,32},{96,64},{0,96},{33,1},{65,33},{97,65},{1,97},{34,2}... | collective-permute-start | bytes 1179656 | tf_op jit(solution)/shard_map/ppermute | solution.py:64
  396.7 9.3 %collective-permute-done.21 = bf16[96,2048]{1,0:T(8,128)(2,1)S(1)} collective-permute-done((bf16[96,2048]{1,0:T(8,128)(2,1)S(1)}, bf16[96,2048]{1,0:T(8,128)(2,1)S(1)}, u32[]{:S(2)}, u32[]{:S(2)}) %collective-permute-start.21) | collective-permute-done | bytes 393248 | tf_op jit(solution)/shard_map/ppermute | solution.py:64
  411.5 16.5 %collective-permute-done.22 = bf16[96,4096]{1,0:T(8,128)(2,1)S(1)} collective-permute-done((bf16[96,4096]{1,0:T(8,128)(2,1)S(1)}, bf16[96,4096]{1,0:T(8,128)(2,1)S(1)}, u32[]{:S(2)}, u32[]{:S(2)}) %collective-permute-start.22) | collective-permute-done | bytes 786464 | tf_op jit(solution)/shard_map/ppermute | solution.py:64
  428.8 10.6 %collective-permute-done.25 = bf16[48,4096]{1,0:T(8,128)(2,1)S(1)} collective-permute-done((bf16[48,4096]{1,0:T(8,128)(2,1)S(1)}, bf16[48,4096]{1,0:T(8,128)(2,1)S(1)}, u32[]{:S(2)}, u32[]{:S(2)}) %collective-permute-start.25) | collective-permute-done | bytes 393248 | tf_op jit(solution)/shard_map/ppermute | solution.py:59
  441.9 3.5 all-to-all-start.4
  449.3 6.9 %all-to-all-done.4 = bf16[8,48,1024]{2,1,0:T(8,128)(2,1)S(1)} async-done(((bf16[8,48,1024]{2,1,0:T(8,128)(2,1)}), bf16[8,48,1024]{2,1,0:T(8,128)(2,1)S(1)}, u32[]{:S(2)}, u32[]{:S(2)}) %all-to-all-start.4) | async-done | bytes 786464 | tf_op jit(solution)/shard_map/all_to_all | solution.py:55
  (186 shorter events, 71.7 us)
Async XLA Ops:
  7.5 21.4 %all-to-all-start = ((bf16[8,64,1024]{2,1,0:T(8,128)(2,1)}), bf16[8,64,1024]{2,1,0:T(8,128)(2,1)S(1)}, u32[]{:S(2)}, u32[]{:S(2)}) async-start(bf16[8,64,1024]{2,1,0:T(8,128)(2,1)} %pad_maximum_fusion.1), calls=%async_computation | async-start | bytes 2097152 | tf_op jit(solution)/shard_map/all_to_all | solution.py:55
  28.9 140.9 %all-to-all-start.1 = ((bf16[16,256,1024]{2,1,0:T(8,128)(2,1)}), bf16[16,256,1024]{2,1,0:T(8,128)(2,1)}, u32[]{:S(2)}, u32[]{:S(2)}) async-start(bf16[16,256,1024]{2,1,0:T(8,128)(2,1)} %shard_map.165), calls=%async_computation.1 | async-start | bytes 16777216 | tf_op jit(solution)/shard_map/all_to_all | solution.py:55
  37.5 3.8 collective-permute-start.1
  41.3 5.3 %collective-permute-start.2 = (f32[18,128]{1,0:T(8,128)S(1)}, f32[18,128]{1,0:T(8,128)S(1)}, u32[]{:S(2)}, u32[]{:S(2)}) collective-permute-start(f32[18,128]{1,0:T(8,128)S(1)} %fusion.64), channel_id=1, source_target_pairs={{0,2},{1,3},{2,0},{3,1},{4,6},{5,7},{6,4},{7,5},{8,10},{9,11},{10,... | collective-permute-start | bytes 27656 | tf_op jit(solution)/shard_map/ppermute | solution.py:59
  46.6 25.3 %collective-permute-start.3 = (f32[18,128]{1,0:T(8,128)S(1)}, f32[18,128]{1,0:T(8,128)S(1)}, u32[]{:S(2)}, u32[]{:S(2)}) collective-permute-start(f32[18,128]{1,0:T(8,128)S(1)} %add.106), channel_id=1, source_target_pairs={{0,4},{1,5},{2,6},{3,7},{4,0},{5,1},{6,2},{7,3},{8,12},{9,13},{10,... | collective-permute-start | bytes 27656 | tf_op jit(solution)/shard_map/ppermute | solution.py:59
  74.9 94.7 %collective-permute-start = (bf16[2,48,4096]{2,1,0:T(8,128)(2,1)S(1)}, bf16[2,48,4096]{2,1,0:T(8,128)(2,1)S(1)}, u32[]{:S(2)}, u32[]{:S(2)}) collective-permute-start(bf16[2,48,4096]{2,1,0:T(8,128)(2,1)S(1)} %constant_dynamic-update-slice_fusion), channel_id=1, source_target_pairs={{0,16},{16,0},{1,17},{17,1},{2,18},{18,2},{3,19},{19,3},{4,20},{20... | collective-permute-start | bytes 2359304 | tf_op jit(solution)/shard_map/ppermute | solution.py:59
  102.0 67.0 %collective-permute-start.4 = (f32[17]{0:T(128)S(1)}, f32[17]{0:T(128)S(1)}, u32[]{:S(2)}, u32[]{:S(2)}) collective-permute-start(f32[17]{0:T(128)S(1)} %pad_maximum_fusion.10), channel_id=1, source_target_pairs={{0,32},{32,0},{64,96},{96,64},{1,33},{33,1},{65,97},{97,65},{2,34}... | collective-permute-start | bytes 212 | tf_op jit(solution)/shard_map/ppermute | solution.py:59
  169.8 37.8 %collective-permute-start.5 = (bf16[2,2,48,4096]{3,2,1,0:T(8,128)(2,1)S(1)}, bf16[2,2,48,4096]{3,2,1,0:T(8,128)(2,1)}, u32[]{:S(2)}, u32[]{:S(2)}) collective-permute-start(bf16[2,2,48,4096]{3,2,1,0:T(8,128)(2,1)S(1)} %pad_maximum_fusion), channel_id=1, source_target_pairs={{32,0},{64,32},{96,64},{0,96},{33,1},{65,33},{97,65},{1,97},{34,2}... | collective-permute-start | bytes 4718600 | tf_op jit(solution)/shard_map/ppermute | solution.py:64
  170.1 40.0 %collective-permute-start.6 = (bf16[2,2,48,4096]{3,2,1,0:T(8,128)(2,1)S(1)}, bf16[2,2,48,4096]{3,2,1,0:T(8,128)(2,1)}, u32[]{:S(2)}, u32[]{:S(2)}) collective-permute-start(bf16[2,2,48,4096]{3,2,1,0:T(8,128)(2,1)S(1)} %pad_maximum_fusion), channel_id=1, source_target_pairs={{64,0},{96,32},{0,64},{32,96},{65,1},{97,33},{1,65},{33,97},{66,2}... | collective-permute-start | bytes 4718600 | tf_op jit(solution)/shard_map/ppermute | solution.py:64
  174.3 68.6 %collective-permute-start.7 = (bf16[2,2,48,4096]{3,2,1,0:T(8,128)(2,1)S(1)}, bf16[2,2,48,4096]{3,2,1,0:T(8,128)(2,1)}, u32[]{:S(2)}, u32[]{:S(2)}) collective-permute-start(bf16[2,2,48,4096]{3,2,1,0:T(8,128)(2,1)S(1)} %pad_maximum_fusion), channel_id=1, source_target_pairs={{96,0},{0,32},{32,64},{64,96},{97,1},{1,33},{33,65},{65,97},{98,2}... | collective-permute-start | bytes 4718600 | tf_op jit(solution)/shard_map/ppermute | solution.py:64
  174.3 71.0 %collective-permute-start.8 = (bf16[2,2,48,4096]{3,2,1,0:T(8,128)(2,1)S(1)}, bf16[2,2,48,4096]{3,2,1,0:T(8,128)(2,1)}, u32[]{:S(2)}, u32[]{:S(2)}) collective-permute-start(bf16[2,2,48,4096]{3,2,1,0:T(8,128)(2,1)S(1)} %pad_maximum_fusion), channel_id=1, source_target_pairs={{0,8},{8,0},{1,9},{9,1},{2,10},{10,2},{3,11},{11,3},{4,12},{12,4},... | collective-permute-start | bytes 4718600 | tf_op jit(solution)/shard_map/ppermute | solution.py:59
  175.4 92.2 %collective-permute-start.13 = (f32[17]{0:T(128)S(1)}, f32[17]{0:T(128)S(1)}, u32[]{:S(2)}, u32[]{:S(2)}) collective-permute-start(f32[17]{0:T(128)S(1)} %fusion.92), channel_id=1, source_target_pairs={{0,64},{32,96},{64,0},{96,32},{1,65},{33,97},{65,1},{97,33},{2,66}... | collective-permute-start | bytes 212 | tf_op jit(solution)/shard_map/ppermute | solution.py:59
  177.6 112.3 %all-to-all-start.2 = ((bf16[16,256,512]{2,1,0:T(8,128)(2,1)}), bf16[16,256,512]{2,1,0:T(8,128)(2,1)}, u32[]{:S(2)}, u32[]{:S(2)}) async-start(bf16[16,256,512]{2,1,0:T(8,128)(2,1)} %get-tuple-element.28), calls=%async_computation.2 | async-start | bytes 8388608 | tf_op jit(solution)/shard_map/all_to_all | solution.py:55
  212.6 35.8 %collective-permute-start.9 = (bf16[2,2,48,4096]{3,2,1,0:T(8,128)(2,1)}, bf16[2,2,48,4096]{3,2,1,0:T(8,128)(2,1)S(1)}, u32[]{:S(2)}, u32[]{:S(2)}) collective-permute-start(bf16[2,2,48,4096]{3,2,1,0:T(8,128)(2,1)} %collective-permute-done.5), channel_id=1, source_target_pairs={{0,8},{8,0},{1,9},{9,1},{2,10},{10,2},{3,11},{11,3},{4,12},{12,4},... | collective-permute-start | bytes 4718600 | tf_op jit(solution)/shard_map/ppermute | solution.py:59
  245.3 4.1 collective-permute-start.10
  247.8 3.8 collective-permute-start.11
  267.0 5.7 %collective-permute-start.12 = (bf16[384,4096]{1,0:T(8,128)(2,1)S(1)}, bf16[384,4096]{1,0:T(8,128)(2,1)S(1)}, u32[]{:S(2)}, u32[]{:S(2)}) collective-permute-start(bf16[384,4096]{1,0:T(8,128)(2,1)S(1)} %convolution_convert_fusion.1), channel_id=1, source_target_pairs={{0,8},{8,0},{1,9},{9,1},{2,10},{10,2},{3,11},{11,3},{4,12},{12,4},... | collective-permute-start | bytes 9437192 | tf_op jit(solution)/shard_map/ppermute | solution.py:59
  290.9 16.1 %collective-permute-start.14 = (bf16[96,2048]{1,0:T(8,128)(2,1)}, bf16[96,2048]{1,0:T(8,128)(2,1)}, u32[]{:S(2)}, u32[]{:S(2)}) collective-permute-start(bf16[96,2048]{1,0:T(8,128)(2,1)} %get-tuple-element.62), channel_id=1, source_target_pairs={{96,0},{0,32},{32,64},{64,96},{97,1},{1,33},{33,65},{65,97},{98,2}... | collective-permute-start | bytes 1179656 | tf_op jit(solution)/shard_map/ppermute | solution.py:64
  292.8 14.2 %collective-permute-start.16 = (bf16[96,2048]{1,0:T(8,128)(2,1)}, bf16[96,2048]{1,0:T(8,128)(2,1)}, u32[]{:S(2)}, u32[]{:S(2)}) collective-permute-start(bf16[96,2048]{1,0:T(8,128)(2,1)} %get-tuple-element.63), channel_id=1, source_target_pairs={{32,0},{64,32},{96,64},{0,96},{33,1},{65,33},{97,65},{1,97},{34,2}... | collective-permute-start | bytes 1179656 | tf_op jit(solution)/shard_map/ppermute | solution.py:64
  294.1 78.1 %all-to-all-start.3 = ((bf16[16,256,512]{2,1,0:T(8,128)(2,1)}), bf16[16,256,512]{2,1,0:T(8,128)(2,1)}, u32[]{:S(2)}, u32[]{:S(2)}) async-start(bf16[16,256,512]{2,1,0:T(8,128)(2,1)} %get-tuple-element.33), calls=%async_computation.3 | async-start | bytes 8388608 | tf_op jit(solution)/shard_map/all_to_all | solution.py:55
  303.6 30.5 %collective-permute-start.18 = (f32[17]{0:T(128)S(1)}, f32[17]{0:T(128)S(1)}, u32[]{:S(2)}, u32[]{:S(2)}) collective-permute-start(f32[17]{0:T(128)S(1)} %add.113), channel_id=1, source_target_pairs={{0,16},{16,0},{1,17},{17,1},{2,18},{18,2},{3,19},{19,3},{4,20},{20... | collective-permute-start | bytes 212 | tf_op jit(solution)/shard_map/ppermute | solution.py:59
  308.5 62.6 %collective-permute-start.15 = (bf16[96,4096]{1,0:T(8,128)(2,1)S(1)}, bf16[96,4096]{1,0:T(8,128)(2,1)S(1)}, u32[]{:S(2)}, u32[]{:S(2)}) collective-permute-start(bf16[96,4096]{1,0:T(8,128)(2,1)S(1)} %pad_maximum_fusion.2), channel_id=1, source_target_pairs={{96,0},{0,32},{32,64},{64,96},{97,1},{1,33},{33,65},{65,97},{98,2}... | collective-permute-start | bytes 2359304 | tf_op jit(solution)/shard_map/ppermute | solution.py:64
  315.4 55.7 %collective-permute-start.17 = (bf16[96,4096]{1,0:T(8,128)(2,1)S(1)}, bf16[96,4096]{1,0:T(8,128)(2,1)S(1)}, u32[]{:S(2)}, u32[]{:S(2)}) collective-permute-start(bf16[96,4096]{1,0:T(8,128)(2,1)S(1)} %pad_maximum_fusion.3), channel_id=1, source_target_pairs={{32,0},{64,32},{96,64},{0,96},{33,1},{65,33},{97,65},{1,97},{34,2}... | collective-permute-start | bytes 2359304 | tf_op jit(solution)/shard_map/ppermute | solution.py:64
  381.2 5.7 %collective-permute-start.20 = (bf16[384,4096]{1,0:T(8,128)(2,1)S(1)}, bf16[384,4096]{1,0:T(8,128)(2,1)S(1)}, u32[]{:S(2)}, u32[]{:S(2)}) collective-permute-start(bf16[384,4096]{1,0:T(8,128)(2,1)S(1)} %convolution_convert_fusion), channel_id=1, source_target_pairs={{0,8},{8,0},{1,9},{9,1},{2,10},{10,2},{3,11},{11,3},{4,12},{12,4},... | collective-permute-start | bytes 9437192 | tf_op jit(solution)/shard_map/ppermute | solution.py:59
  388.9 17.2 %collective-permute-start.21 = (bf16[96,2048]{1,0:T(8,128)(2,1)S(1)}, bf16[96,2048]{1,0:T(8,128)(2,1)S(1)}, u32[]{:S(2)}, u32[]{:S(2)}) collective-permute-start(bf16[96,2048]{1,0:T(8,128)(2,1)S(1)} %get-tuple-element.56), channel_id=1, source_target_pairs={{96,0},{0,32},{32,64},{64,96},{97,1},{1,33},{33,65},{65,97},{98,2}... | collective-permute-start | bytes 1179656 | tf_op jit(solution)/shard_map/ppermute | solution.py:64
  391.4 16.2 %collective-permute-start.23 = (bf16[96,2048]{1,0:T(8,128)(2,1)S(1)}, bf16[96,2048]{1,0:T(8,128)(2,1)S(1)}, u32[]{:S(2)}, u32[]{:S(2)}) collective-permute-start(bf16[96,2048]{1,0:T(8,128)(2,1)S(1)} %get-tuple-element.57), channel_id=1, source_target_pairs={{32,0},{64,32},{96,64},{0,96},{33,1},{65,33},{97,65},{1,97},{34,2}... | collective-permute-start | bytes 1179656 | tf_op jit(solution)/shard_map/ppermute | solution.py:64
  408.0 20.0 %collective-permute-start.22 = (bf16[96,4096]{1,0:T(8,128)(2,1)S(1)}, bf16[96,4096]{1,0:T(8,128)(2,1)S(1)}, u32[]{:S(2)}, u32[]{:S(2)}) collective-permute-start(bf16[96,4096]{1,0:T(8,128)(2,1)S(1)} %pad_maximum_fusion.4), channel_id=1, source_target_pairs={{96,0},{0,32},{32,64},{64,96},{97,1},{1,33},{33,65},{65,97},{98,2}... | collective-permute-start | bytes 2359304 | tf_op jit(solution)/shard_map/ppermute | solution.py:64
  409.9 18.2 %collective-permute-start.24 = (bf16[96,4096]{1,0:T(8,128)(2,1)S(1)}, bf16[96,4096]{1,0:T(8,128)(2,1)S(1)}, u32[]{:S(2)}, u32[]{:S(2)}) collective-permute-start(bf16[96,4096]{1,0:T(8,128)(2,1)S(1)} %pad_maximum_fusion.5), channel_id=1, source_target_pairs={{32,0},{64,32},{96,64},{0,96},{33,1},{65,33},{97,65},{1,97},{34,2}... | collective-permute-start | bytes 2359304 | tf_op jit(solution)/shard_map/ppermute | solution.py:64
  411.4 17.0 %collective-permute-start.19 = (bf16[48,4096]{1,0:T(8,128)(2,1)S(1)}, bf16[48,4096]{1,0:T(8,128)(2,1)S(1)}, u32[]{:S(2)}, u32[]{:S(2)}) collective-permute-start(bf16[48,4096]{1,0:T(8,128)(2,1)S(1)} %slice.225), channel_id=1, source_target_pairs={{0,16},{16,0},{1,17},{17,1},{2,18},{18,2},{3,19},{19,3},{4,20},{20... | collective-permute-start | bytes 1179656 | tf_op jit(solution)/shard_map/ppermute | solution.py:59
  428.4 10.9 %collective-permute-start.25 = (bf16[48,4096]{1,0:T(8,128)(2,1)S(1)}, bf16[48,4096]{1,0:T(8,128)(2,1)S(1)}, u32[]{:S(2)}, u32[]{:S(2)}) collective-permute-start(bf16[48,4096]{1,0:T(8,128)(2,1)S(1)} %slice.286), channel_id=1, source_target_pairs={{0,16},{16,0},{1,17},{17,1},{2,18},{18,2},{3,19},{19,3},{4,20},{20... | collective-permute-start | bytes 1179656 | tf_op jit(solution)/shard_map/ppermute | solution.py:59
  441.9 14.2 %all-to-all-start.4 = ((bf16[8,48,1024]{2,1,0:T(8,128)(2,1)}), bf16[8,48,1024]{2,1,0:T(8,128)(2,1)S(1)}, u32[]{:S(2)}, u32[]{:S(2)}) async-start(bf16[8,48,1024]{2,1,0:T(8,128)(2,1)} %reshape.333), calls=%async_computation.4 | async-start | bytes 1572864 | tf_op jit(solution)/shard_map/all_to_all | solution.py:55
  445.5 1.2 collective-permute-start.26
  (17 other events, 299.0 us)

commit v2 on v1

v2 whole, which is shorter than its diff:
```python
import jax
import jax.numpy as jnp
from jax import lax
from jax.experimental import pallas as pl
from jax.sharding import Mesh
from jax.sharding import PartitionSpec as P

D = 4096
SEG = 32
ROW = "dp_y"
COLUMN = "dp_z"
CORE = "dp_core"
DP = (ROW, COLUMN, CORE)


EPSILON = 1e-05
KL_WEIGHT = 1.0
BALANCE_WEIGHT = 0.5
PACK = 2


def pack_kernel(*refs):
    packed_ref = refs[-1]
    piece = refs[0].shape[1] // PACK
    for k in range(PACK):
        for place, ref in enumerate(refs[:-1]):
            packed_ref[k, :, place * piece : (place + 1) * piece] = ref[
                :, k * piece : (k + 1) * piece
            ]


def packed(weights, peers):
    rows, width = weights[0].shape[1:]
    piece = width // peers
    taken = pl.BlockSpec((None, rows, PACK * piece), lambda j: (0, 0, j))
    wide = len(weights) * piece
    return pl.pallas_call(
        pack_kernel,
        grid=(peers // PACK,),
        in_specs=[taken] * len(weights),
        out_specs=pl.BlockSpec((PACK, rows, wide), lambda j: (j, 0, 0)),
        out_shape=jax.ShapeDtypeStruct((peers, rows, wide), weights[0].dtype),
        cost_estimate=pl.CostEstimate(
            flops=0, bytes_accessed=4 * len(weights) * rows * width, transcendentals=0
        ),
    )(*weights)


def router_terms(hidden, norm_gain, router):
    values = hidden.astype(jnp.float32)
    partial_logits = jnp.dot(values * norm_gain, router, precision=lax.Precision.HIGHEST)
    return (partial_logits, jnp.sum(values * values, axis=1))


def exchange(value, axis):
    return lax.all_to_all(value, axis, split_axis=0, concat_axis=0, tiled=True)


def from_xor(value, axis, step):
    return lax.ppermute(value, axis, [(i, i ^ step) for i in range(lax.axis_size(axis))])


def from_ahead(value, axis, step):
    size = lax.axis_size(axis)
    return lax.ppermute(value, axis, [((i + step) % size, i) for i in range(size)])


def of_everyone(value, *axes):
    for axis in axes:
        step = 1
        while step < lax.axis_size(axis):
            value = value + from_xor(value, axis, step)
            step *= 2
    return value


def row_blocks(own):
    ahead, behind, far = (from_ahead(own, ROW, k) for k in (1, 3, 2))
    return (own, ahead, far, behind)


def gathered(policy_own, reference_own):
    pair = jnp.stack((policy_own, from_xor(policy_own, COLUMN, 1)))
    row = jnp.stack(row_blocks(reference_own))
    columns = (row, from_xor(row, COLUMN, 1))
    return (both_cores(row_blocks(pair)), columns)


def both_cores(pieces):
    pieces = (*pieces, *(from_xor(piece, CORE, 1) for piece in pieces))
    return jnp.concatenate([piece.reshape(-1, piece.shape[-1]) for piece in pieces])


def split_in_three(values):
    rows = []
    for _ in range(3):
        rounded = lax.reduce_precision(values, exponent_bits=8, mantissa_bits=7)
        rows.append(rounded.astype(jnp.bfloat16))
        values = values - rounded
    return jnp.stack(rows)


def normed_rows(arrived, gain):
    values = arrived.astype(jnp.float32)
    scale = lax.rsqrt(jnp.sum(values * values, axis=(0, 2)) / D + EPSILON)
    normed = (values * gain[:, None, :] * scale[None, :, None]).astype(jnp.bfloat16)
    return normed.transpose(1, 0, 2).reshape(arrived.shape[1], -1)


def hidden_units(rows, gate_up):
    both = jnp.dot(rows, gate_up, preferred_element_type=jnp.float32)
    width = both.shape[1] // 2
    return (jax.nn.silu(both[:, :width]) * both[:, width:]).astype(jnp.bfloat16)


def added(*terms):
    total = terms[0].astype(jnp.float32)
    for term in terms[1:]:
        total = total + term.astype(jnp.float32)
    return total.astype(jnp.bfloat16)


def core_terms(hidden, down):
    return jnp.dot(hidden, down, preferred_element_type=jnp.float32)


def chip_terms(mine, sent):
    return added(mine, from_xor(sent, CORE, 1)).reshape(lax.axis_size(ROW), -1, mine.shape[1])


def from_two_away(chip):
    middle = chip.shape[2] // 2
    return (from_ahead(chip[2, :, :middle], ROW, 3), from_ahead(chip[2, :, middle:], ROW, 1))


def toward_neighbours(chip, left, right):
    middle = chip.shape[2] // 2
    ahead = jnp.concatenate((added(chip[1, :, :middle], left), chip[1, :, middle:]), axis=1)
    behind = jnp.concatenate((chip[3, :, :middle], added(chip[3, :, middle:], right)), axis=1)
    return (ahead, behind)


def row_terms(own, ahead, behind):
    return added(own, from_ahead(ahead, ROW, 3), from_ahead(behind, ROW, 1))


def column_terms(row):
    half = row.shape[0] // 2
    return added(row[:half], from_xor(row[half:], COLUMN, 1))


def per_device(
    policy_hidden,
    reference_hidden,
    policy_norm_gain,
    reference_norm_gain,
    policy_router,
    reference_router,
    policy_gate,
    policy_up,
    policy_down,
    reference_gate,
    reference_up,
    reference_down,
    expert_ids,
    lengths,
):
    expert_count = lax.axis_size("expert")
    peers = lax.axis_size(DP)
    token_count, feature_block = policy_hidden.shape
    route_count = expert_ids.shape[1]
    slot_count = 3 * token_count // expert_count
    token_total = float(token_count * peers)

    policy_partial, policy_squares = router_terms(policy_hidden, policy_norm_gain, policy_router)
    reference_partial, reference_squares = router_terms(
        reference_hidden, reference_norm_gain, reference_router
    )
    sums = jnp.concatenate(
        (policy_partial.T, reference_partial.T, policy_squares[None], reference_squares[None])
    )

    flat_ids = expert_ids.reshape(-1)
    onehot = (flat_ids[:, None] == jnp.arange(expert_count, dtype=jnp.int32)[None, :]).astype(
        jnp.int32
    )
    before = jnp.cumsum(onehot, axis=0) - onehot
    within = jnp.sum(before * onehot, axis=1)
    slot_index = jnp.arange(expert_count * slot_count, dtype=jnp.int32)
    target = (flat_ids * slot_count + within).reshape(token_count, route_count)
    select = jnp.any(slot_index[:, None, None] == target[None, :, :], axis=2)
    placed = jnp.dot(
        select.astype(jnp.bfloat16),
        jnp.concatenate((policy_hidden, reference_hidden), axis=1),
        preferred_element_type=jnp.float32,
    ).astype(jnp.bfloat16)
    small = jnp.concatenate((policy_norm_gain, reference_norm_gain, sums.ravel()))
    small_rows = -(-small.size // (2 * feature_block))
    small = jnp.pad(small, (0, small_rows * 2 * feature_block - small.size))
    small = split_in_three(small.reshape(small_rows, -1)).reshape(3 * small_rows, -1)
    small = jnp.pad(small, ((0, -3 * small_rows % 16), (0, 0)))
    arrived = exchange(
        jnp.concatenate(
            (
                placed.reshape(expert_count, slot_count, 2 * feature_block),
                jnp.broadcast_to(small, (expert_count, *small.shape)),
            ),
            axis=1,
        ),
        "expert",
    )
    weights = packed((policy_gate, policy_up, reference_gate, reference_up), peers)
    arrived, weights = lax.optimization_barrier((arrived, weights))
    small = arrived[:, slot_count : slot_count + 3 * small_rows].astype(jnp.float32)
    small = jnp.sum(small.reshape(expert_count, 3, -1), axis=1)
    gains = small[:, : 2 * feature_block]
    sums = jnp.sum(small[:, 2 * feature_block : 2 * feature_block + sums.size], axis=0)
    arrived = arrived[:, :slot_count]
    policy_rows, reference_columns = gathered(
        normed_rows(arrived[:, :, :feature_block], gains[:, :feature_block]),
        normed_rows(arrived[:, :, feature_block:], gains[:, feature_block:]),
    )
    sums = sums.reshape(2 * expert_count + 2, token_count).T
    policy_scale = lax.rsqrt(sums[:, 2 * expert_count] / D + EPSILON)[:, None]
    reference_scale = lax.rsqrt(sums[:, 2 * expert_count + 1] / D + EPSILON)[:, None]
    policy_logits = sums[:, :expert_count] * policy_scale
    reference_logits = sums[:, expert_count : 2 * expert_count] * reference_scale
    live_mask = (
        (jnp.arange(SEG, dtype=jnp.int32)[None, :] < lengths[:, None])
        .reshape(-1)
        .astype(jnp.float32)
    )
    chosen_slot = target[:, :, None] == slot_index[None, None, :]

    def slot_weights(logits):
        matches = expert_ids[:, :, None] == jnp.arange(expert_count, dtype=jnp.int32)[None, None, :]
        chosen = jnp.sum(jnp.where(matches, logits[:, None, :], 0.0), axis=2)
        gates = jax.nn.softmax(chosen, axis=1) * live_mask[:, None]
        return jnp.sum(jnp.where(chosen_slot, gates[:, :, None], 0.0), axis=1)

    policy_weights = slot_weights(policy_logits)
    reference_weights = slot_weights(reference_logits)
    policy_logprob = jax.nn.log_softmax(policy_logits, axis=1)
    reference_logprob = jax.nn.log_softmax(reference_logits, axis=1)
    policy_prob = jnp.exp(policy_logprob)
    token_kl = jnp.sum(policy_prob * (policy_logprob - reference_logprob), axis=1) * live_mask
    route_onehot = onehot.reshape(token_count, route_count, expert_count)
    counts = jnp.sum(jnp.sum(route_onehot, axis=1).astype(jnp.float32) * live_mask[:, None], axis=0)
    probsum = jnp.sum(policy_prob * live_mask[:, None], axis=0)
    local_totals = jnp.concatenate((counts, probsum, jnp.sum(token_kl)[None]))

    (
        policy_rows,
        reference_columns,
        policy_weights,
        reference_weights,
        token_kl,
        local_totals,
        weights,
    ) = lax.optimization_barrier(
        (
            policy_rows,
            reference_columns,
            policy_weights,
            reference_weights,
            token_kl,
            local_totals,
            weights,
        )
    )
    gate_up = exchange(weights, DP).reshape(D, -1)
    (
        gate_up,
        policy_rows,
        reference_columns,
        policy_weights,
        reference_weights,
        token_kl,
        local_totals,
    ) = lax.optimization_barrier(
        (
            gate_up,
            policy_rows,
            reference_columns,
            policy_weights,
            reference_weights,
            token_kl,
            local_totals,
        )
    )
    width = policy_down.shape[1]
    half = policy_rows.shape[0] // 2
    policy_units = hidden_units(policy_rows, gate_up[:, : 2 * width])
    policy_sent = core_terms(policy_units[half:], policy_down[0]).astype(jnp.bfloat16)
    policy_chip = chip_terms(core_terms(policy_units[:half], policy_down[0]), policy_sent)
    policy_chip, reference_columns = lax.optimization_barrier((policy_chip, reference_columns))
    reference_units = hidden_units(both_cores(reference_columns), gate_up[:, 2 * width :])
    reference_units = reference_units.reshape(
        lax.axis_size(CORE), lax.axis_size(COLUMN), lax.axis_size(ROW), slot_count, width
    )
    reference_units = reference_units.swapaxes(1, 2).reshape(-1, width)
    totals = local_totals + from_xor(local_totals, ROW, 1)
    passing, reference_units, totals = lax.optimization_barrier(
        (from_two_away(policy_chip), reference_units, totals)
    )
    policy_row = row_terms(policy_chip[0], *toward_neighbours(policy_chip, *passing))
    reference_sent = core_terms(reference_units[half:], reference_down[0]).astype(jnp.bfloat16)
    reference_chip = chip_terms(
        core_terms(reference_units[:half], reference_down[0]), reference_sent
    )

    totals = totals + from_xor(totals, ROW, 2)
    reference_chip, totals = lax.optimization_barrier((reference_chip, totals))
    totals = of_everyone(totals, COLUMN, CORE)
    counts, probsum = totals[:expert_count], totals[expert_count : 2 * expert_count]
    kl_total = totals[2 * expert_count]
    balance = expert_count * jnp.sum(counts / (route_count * token_total) * probsum / token_total)
    loss = KL_WEIGHT * kl_total / token_total + BALANCE_WEIGHT * balance
    def mixture(weights, output):
        output = output.reshape(slot_count, expert_count, feature_block).swapaxes(0, 1)
        output = exchange(output, "expert").reshape(expert_count * slot_count, -1)
        mixed = jnp.dot(weights, output.astype(jnp.float32), precision=lax.Precision.HIGHEST)
        return mixed.astype(jnp.bfloat16)

    policy_mixture = mixture(policy_weights, column_terms(policy_row))
    reference_row = row_terms(reference_chip[0], *toward_neighbours(reference_chip, *from_two_away(reference_chip)))
    reference_row, policy_mixture, reference_weights, loss = lax.optimization_barrier(
        (reference_row, policy_mixture, reference_weights, loss)
    )
    reference_mixture = mixture(reference_weights, column_terms(reference_row))
    return (policy_mixture, reference_mixture, token_kl, loss)


def solution(mesh):
    split = Mesh(mesh.devices.reshape(4, 2, 2, mesh.shape["expert"]), (*DP, "expert"))
    placed = (
        P(DP, "expert"),
        P(DP, "expert"),
        P("expert"),
        P("expert"),
        P("expert", None),
        P("expert", None),
        P("expert", DP, None),
        P("expert", DP, None),
        P("expert", DP, None),
        P("expert", DP, None),
        P("expert", DP, None),
        P("expert", DP, None),
        P(DP, None),
        P(DP),
    )
    return jax.shard_map(
        per_device,
        mesh=split,
        in_specs=placed,
        out_specs=(P(DP, "expert"), P(DP, "expert"), P(DP), P()),
        check_vma=False,
    )
```

time: 460 us -> 416 us (0.904)
  blocking collectives: 0 us -> 205 us
  waiting for transfers between devices: 259 us -> 87.5 us
  starting transfers between devices: 105 us -> 43.7 us
  local copies, waits for them, and re-layouts: 27 us -> 11.2 us
    all_to_all x0 -> x2, blocking collectives: none -> 205 us  [exchange(): return lax.all_to_all(value, axis, split_axis=0, concat_axis=0, tiled=True)]
    ppermute x16, waiting for transfers between devices: 109 us -> 31.2 us  [from_xor(): lax.ppermute(value, axis, [(i, i ^ step) for i in range(lax.axis_size(axi...]
    ppermute x11 -> x14, waiting for transfers between devices: 119 us -> 51.6 us  [from_ahead(): lax.ppermute(value, axis, [((i + step) % size, i) for i in range(size)])]
    ppermute x16, starting transfers between devices: 49 us -> 15.6 us  [from_xor(): lax.ppermute(value, axis, [(i, i ^ step) for i in range(lax.axis_size(axi...]
    all_to_all x5 -> x2, waiting for transfers between devices: 30.7 us -> 4.66 us  [exchange(): return lax.all_to_all(value, axis, split_axis=0, concat_axis=0, tiled=True)]
    all_to_all x5 -> x2, starting transfers between devices: 30 us -> 9.19 us  [exchange(): return lax.all_to_all(value, axis, split_axis=0, concat_axis=0, tiled=True)]
    slice x9 -> x1, local copies, waits for them, and re-layouts: 7.62 us -> 0.21 us  [the longest x8 7.41 us: gathered(): piece[:, m].reshape(-1, width)]
    dot_general x3 -> x2, matrix products: 24.7 us -> 17.3 us  [hidden_units(): both = jnp.dot(rows, gate_up, preferred_element_type=jnp.float32)]
  transfers between devices with their start and end apart: 32 -> 32, of which waited for: 20 -> 17; matrix products, arithmetic and copies ran while one was open for 11% -> 6% of each run, Pallas kernels for 3% -> 3%
where the time goes in v2:
time: 416 us; the launch traced here: 415 us
  blocking collectives  205 us (49%)
  waiting for transfers between devices  87.5 us (21%)
  starting transfers between devices  43.7 us (11%)
  matrix products  33.8 us (8%)
  other arithmetic  16.2 us (4%)
  Pallas kernels  13.6 us (3%)
  local copies, waits for them, and re-layouts  11.2 us (3%)
    all_to_all x2, blocking collectives, exchange(): return lax.all_to_all(value, axis, split_axis=0, concat_axis=0, tiled=True)  205 us
    ppermute x14, waiting for transfers between devices, from_ahead(): lax.ppermute(value, axis, [((i + step) % size, i) for i in range(size)])  51.6 us
    ppermute x16, waiting for transfers between devices, from_xor(): lax.ppermute(value, axis, [(i, i ^ step) for i in range(lax.axis_size(axi...  31.2 us
    ppermute x14, starting transfers between devices, from_ahead(): lax.ppermute(value, axis, [((i + step) % size, i) for i in range(size)])  18.9 us
    dot_general x2, matrix products, hidden_units(): both = jnp.dot(rows, gate_up, preferred_element_type=jnp.float32)  17.3 us
    ppermute x16, starting transfers between devices, from_xor(): lax.ppermute(value, axis, [(i, i ^ step) for i in range(lax.axis_size(axi...  15.6 us
    pallas_call x1, Pallas kernels, packed(): pl.pallas_call(pack_kernel, grid=(peers // PACK,), in_specs=[taken] * len...  13.6 us
    dot_general x4, matrix products, core_terms(): return jnp.dot(hidden, down, preferred_element_type=jnp.float32)  9.73 us
  transfers between devices with their start and end apart: 32, of which 17 were waited for; matrix products, arithmetic and copies ran while one was open for 6% of the time, Pallas kernels for 3%

profile of v2, /device:TPU:0, one launch (start us, length us, event | category | flops | bytes accessed | tf_op | source)
XLA Modules:
  0.0 414.9 jit_solution(12981835210023509929)
XLA Ops:
  11.4 5.7 %all-to-all-start = ((bf16[8,64,1024]{2,1,0:T(8,128)(2,1)}), bf16[8,64,1024]{2,1,0:T(8,128)(2,1)S(1)}, u32[]{:S(2)}, u32[]{:S(2)}) async-start(bf16[8,64,1024]{2,1,0:T(8,128)(2,1)} %pad_maximum_fusion.1), calls=%async_computation | async-start | bytes 2097152 | tf_op jit(solution)/shard_map/all_to_all | solution.py:56
  17.3 13.6 %shard_map.165 = bf16[16,256,2048]{2,1,0:T(8,128)(2,1)} custom-call(bf16[1,256,8192]{2,1,0:T(8,128)(2,1)} %refs_0_.1, bf16[1,256,8192]{2,1,0:T(8,128)(2,1)} %refs_1_.1, bf16[1,256,8192]{2,1,0:T(8,128)(2,1)} %refs_2_.1, bf16[1,256,8192]{2,1,0:T(8,128)(2,1)} %refs_3_.1), custom_call_target="tpu_custom_call" | custom-call | bytes 33554432 | tf_op jit(solution)/shard_map/pallas_call | solution.py:37
  30.9 1.9 all-to-all-done
  36.6 2.9 collective-permute-start.9
  43.0 3.6 collective-permute-start
  49.1 5.8 %collective-permute-done = bf16[48,4096]{1,0:T(8,128)(2,1)S(1)} collective-permute-done((bf16[48,4096]{1,0:T(8,128)(2,1)}, bf16[48,4096]{1,0:T(8,128)(2,1)S(1)}, u32[]{:S(2)}, u32[]{:S(2)}) %collective-permute-start) | collective-permute-done | bytes 393248 | tf_op jit(solution)/shard_map/ppermute | solution.py:60
  58.8 3.3 collective-permute-start.11
  62.2 29.5 %collective-permute-done.2 = bf16[2,48,4096]{2,1,0:T(8,128)(2,1)S(1)} collective-permute-done((bf16[2,48,4096]{2,1,0:T(8,128)(2,1)S(1)}, bf16[2,48,4096]{2,1,0:T(8,128)(2,1)S(1)}, u32[]{:S(2)}, u32[]{:S(2)}) %collective-permute-start.2) | collective-permute-done | bytes 786464 | tf_op jit(solution)/shard_map/ppermute | solution.py:65
  91.7 2.0 collective-permute-done.1
  97.2 2.6 copy-done.5
  99.9 193.1 %all_to_all.20 = bf16[16,256,2048]{2,1,0:T(8,128)(2,1)S(1)} all-to-all(bf16[16,256,2048]{2,1,0:T(8,128)(2,1)S(1)} %copy-done.2), channel_id=1, replica_groups=mesh['dp_y'=4,'dp_z'=2,'dp_core'=2,'expert'=8] {'dp_y','dp_z','dp_core'}, dimensions={0} | all-to-all | bytes 33554432 | tf_op jit(solution)/shard_map/all_to_all | solution.py:56
  292.9 6.8 %fusion.2 = f32[768,1024]{1,0:T(8,128)S(1)} fusion(bf16[768,4096]{1,0:T(8,128)(2,1)S(1)} %copy-done.6, bf16[4096,2048]{1,0:T(8,128)(2,1)S(1)} %bitcast.123), kind=kOutput, calls=%fused_computation.2 | convolution fusion | flops 6442450944 | bytes 17825792 | tf_op jit(solution)/shard_map/dot_general | solution.py:111
  300.3 4.2 %convolution_convert_fusion.1 = bf16[384,4096]{1,0:T(8,128)(2,1)S(1)} fusion(bf16[1,512,4096]{2,1,0:T(8,128)(2,1)} %param.23, bf16[768,512]{1,0:T(8,128)(2,1)S(1)} %fusion.19), kind=kOutput, calls=%fused_computation.14 | convolution fusion | flops 1612185600 | bytes 7733248 | tf_op jit(solution)/shard_map/dot_general | solution.py:124
  304.6 5.6 %collective-permute-done.12 = bf16[384,4096]{1,0:T(8,128)(2,1)S(1)} collective-permute-done((bf16[384,4096]{1,0:T(8,128)(2,1)S(1)}, bf16[384,4096]{1,0:T(8,128)(2,1)S(1)}, u32[]{:S(2)}, u32[]{:S(2)}) %collective-permute-start.12) | collective-permute-done | bytes 3145760 | tf_op jit(solution)/shard_map/ppermute | solution.py:60
  310.2 1.9 add_convert_fusion.1
  312.8 3.5 collective-permute-done.17
  318.6 10.5 %fusion = f32[768,1024]{1,0:T(8,128)S(1)} fusion(bf16[4096,2048]{1,0:T(8,128)(2,1)} %bitcast.124, bf16[192,4096]{1,0:T(8,128)(2,1)} %bitcast.36, bf16[192,4096]{1,0:T(8,128)(2,1)S(1)} %bitcast.159, bf16[192,4096]{1,0:T(8,128)(2,1)S(1)} %bitcast.158, bf16[192,4096]{1,0:T(8,128)(2,1)S(1)} %bitcast.134), kind=kOutput, calls=%fused_computation | convolution fusion | flops 6467616768 | bytes 17825792 | tf_op jit(solution)/shard_map/dot_general | solution.py:111
  338.8 1.8 add_convert_fusion
  340.9 3.2 collective-permute-start.22
  344.1 10.9 %collective-permute-done.25 = bf16[96,4096]{1,0:T(8,128)(2,1)S(1)} collective-permute-done((bf16[96,4096]{1,0:T(8,128)(2,1)S(1)}, bf16[96,4096]{1,0:T(8,128)(2,1)S(1)}, u32[]{:S(2)}, u32[]{:S(2)}) %collective-permute-start.25) | collective-permute-done | bytes 786464 | tf_op jit(solution)/shard_map/ppermute | solution.py:65
  355.0 3.1 collective-permute-done.24
  358.4 2.0 collective-permute-start.26
  360.5 4.9 %collective-permute-done.20 = bf16[96,2048]{1,0:T(8,128)(2,1)S(1)} collective-permute-done((bf16[96,2048]{1,0:T(8,128)(2,1)S(1)}, bf16[96,2048]{1,0:T(8,128)(2,1)S(1)}, u32[]{:S(2)}, u32[]{:S(2)}) %collective-permute-start.20) | collective-permute-done | bytes 393248 | tf_op jit(solution)/shard_map/ppermute | solution.py:65
  367.8 1.8 collective-permute-start.21
  370.7 3.5 all-to-all-start.2
  374.2 2.0 collective-permute-start.27
  376.2 3.1 collective-permute-done.27
  379.4 2.7 all-to-all-done.2
  382.1 2.0 convolution_convert_fusion.4
  389.5 2.0 collective-permute-start.29
  391.5 8.6 %collective-permute-done.29 = bf16[48,4096]{1,0:T(8,128)(2,1)S(1)} collective-permute-done((bf16[48,4096]{1,0:T(8,128)(2,1)S(1)}, bf16[48,4096]{1,0:T(8,128)(2,1)S(1)}, u32[]{:S(2)}, u32[]{:S(2)}) %collective-permute-start.29) | collective-permute-done | bytes 393248 | tf_op jit(solution)/shard_map/ppermute | solution.py:60
  400.5 12.2 %all_to_all.21 = bf16[8,48,512]{2,1,0:T(8,128)(2,1)S(1)} all-to-all(bf16[8,48,512]{2,1,0:T(8,128)(2,1)S(1)} %copy.81), channel_id=1, replica_groups=mesh['dp_y'=4,'dp_z'=2,'dp_core'=2,'expert'=8] {'expert'}, dimensions={0} | all-to-all | bytes 786432 | tf_op jit(solution)/shard_map/all_to_all | solution.py:56
  (165 shorter events, 50.5 us)
Async XLA Ops:
  11.4 21.4 %all-to-all-start = ((bf16[8,64,1024]{2,1,0:T(8,128)(2,1)}), bf16[8,64,1024]{2,1,0:T(8,128)(2,1)S(1)}, u32[]{:S(2)}, u32[]{:S(2)}) async-start(bf16[8,64,1024]{2,1,0:T(8,128)(2,1)} %pad_maximum_fusion.1), calls=%async_computation | async-start | bytes 2097152 | tf_op jit(solution)/shard_map/all_to_all | solution.py:56
  35.0 20.8 %collective-permute-start.10 = (bf16[48,4096]{1,0:T(8,128)(2,1)}, bf16[48,4096]{1,0:T(8,128)(2,1)S(1)}, u32[]{:S(2)}, u32[]{:S(2)}) collective-permute-start(bf16[48,4096]{1,0:T(8,128)(2,1)} %bitcast.70), channel_id=1, source_target_pairs={{96,0},{0,32},{32,64},{64,96},{97,1},{1,33},{33,65},{65,97},{98,2}... | collective-permute-start | bytes 1179656 | tf_op jit(solution)/shard_map/ppermute | solution.py:65
  36.6 20.9 %collective-permute-start.9 = (bf16[48,4096]{1,0:T(8,128)(2,1)}, bf16[48,4096]{1,0:T(8,128)(2,1)S(1)}, u32[]{:S(2)}, u32[]{:S(2)}) collective-permute-start(bf16[48,4096]{1,0:T(8,128)(2,1)} %bitcast.70), channel_id=1, source_target_pairs={{64,0},{96,32},{0,64},{32,96},{65,1},{97,33},{1,65},{33,97},{66,2}... | collective-permute-start | bytes 1179656 | tf_op jit(solution)/shard_map/ppermute | solution.py:65
  39.5 19.1 %collective-permute-start.8 = (bf16[48,4096]{1,0:T(8,128)(2,1)}, bf16[48,4096]{1,0:T(8,128)(2,1)S(1)}, u32[]{:S(2)}, u32[]{:S(2)}) collective-permute-start(bf16[48,4096]{1,0:T(8,128)(2,1)} %bitcast.70), channel_id=1, source_target_pairs={{32,0},{64,32},{96,64},{0,96},{33,1},{65,33},{97,65},{1,97},{34,2}... | collective-permute-start | bytes 1179656 | tf_op jit(solution)/shard_map/ppermute | solution.py:65
  43.0 11.9 %collective-permute-start = (bf16[48,4096]{1,0:T(8,128)(2,1)}, bf16[48,4096]{1,0:T(8,128)(2,1)S(1)}, u32[]{:S(2)}, u32[]{:S(2)}) collective-permute-start(bf16[48,4096]{1,0:T(8,128)(2,1)} %bitcast.68), channel_id=1, source_target_pairs={{0,16},{16,0},{1,17},{17,1},{2,18},{18,2},{3,19},{19,3},{4,20},{20... | collective-permute-start | bytes 1179656 | tf_op jit(solution)/shard_map/ppermute | solution.py:60
  55.0 38.9 %collective-permute-start.4 = (bf16[2,48,4096]{2,1,0:T(8,128)(2,1)S(1)}, bf16[2,48,4096]{2,1,0:T(8,128)(2,1)S(1)}, u32[]{:S(2)}, u32[]{:S(2)}) collective-permute-start(bf16[2,48,4096]{2,1,0:T(8,128)(2,1)S(1)} %pad_maximum_fusion.2), channel_id=1, source_target_pairs={{0,8},{8,0},{1,9},{9,1},{2,10},{10,2},{3,11},{11,3},{4,12},{12,4},... | collective-permute-start | bytes 2359304 | tf_op jit(solution)/shard_map/ppermute | solution.py:60
  55.1 38.8 %collective-permute-start.3 = (bf16[2,48,4096]{2,1,0:T(8,128)(2,1)S(1)}, bf16[2,48,4096]{2,1,0:T(8,128)(2,1)S(1)}, u32[]{:S(2)}, u32[]{:S(2)}) collective-permute-start(bf16[2,48,4096]{2,1,0:T(8,128)(2,1)S(1)} %pad_maximum_fusion.2), channel_id=1, source_target_pairs={{96,0},{0,32},{32,64},{64,96},{97,1},{1,33},{33,65},{65,97},{98,2}... | collective-permute-start | bytes 2359304 | tf_op jit(solution)/shard_map/ppermute | solution.py:65
  55.8 35.9 %collective-permute-start.2 = (bf16[2,48,4096]{2,1,0:T(8,128)(2,1)S(1)}, bf16[2,48,4096]{2,1,0:T(8,128)(2,1)S(1)}, u32[]{:S(2)}, u32[]{:S(2)}) collective-permute-start(bf16[2,48,4096]{2,1,0:T(8,128)(2,1)S(1)} %pad_maximum_fusion.2), channel_id=1, source_target_pairs={{64,0},{96,32},{0,64},{32,96},{65,1},{97,33},{1,65},{33,97},{66,2}... | collective-permute-start | bytes 2359304 | tf_op jit(solution)/shard_map/ppermute | solution.py:65
  57.5 36.2 %collective-permute-start.1 = (bf16[2,48,4096]{2,1,0:T(8,128)(2,1)S(1)}, bf16[2,48,4096]{2,1,0:T(8,128)(2,1)S(1)}, u32[]{:S(2)}, u32[]{:S(2)}) collective-permute-start(bf16[2,48,4096]{2,1,0:T(8,128)(2,1)S(1)} %pad_maximum_fusion.2), channel_id=1, source_target_pairs={{32,0},{64,32},{96,64},{0,96},{33,1},{65,33},{97,65},{1,97},{34,2}... | collective-permute-start | bytes 2359304 | tf_op jit(solution)/shard_map/ppermute | solution.py:65
  58.8 38.4 %collective-permute-start.11 = (bf16[4,48,4096]{2,1,0:T(8,128)(2,1)S(1)}, bf16[4,48,4096]{2,1,0:T(8,128)(2,1)S(1)}, u32[]{:S(2)}, u32[]{:S(2)}) collective-permute-start(bf16[4,48,4096]{2,1,0:T(8,128)(2,1)S(1)} %pad_maximum_fusion), channel_id=1, source_target_pairs={{0,16},{16,0},{1,17},{17,1},{2,18},{18,2},{3,19},{19,3},{4,20},{20... | collective-permute-start | bytes 4718600 | tf_op jit(solution)/shard_map/ppermute | solution.py:60
  91.7 4.4 %collective-permute-start.6 = (bf16[2,48,4096]{2,1,0:T(8,128)(2,1)S(1)}, bf16[2,48,4096]{2,1,0:T(8,128)(2,1)S(1)}, u32[]{:S(2)}, u32[]{:S(2)}) collective-permute-start(bf16[2,48,4096]{2,1,0:T(8,128)(2,1)S(1)} %collective-permute-done.2), channel_id=1, source_target_pairs={{0,8},{8,0},{1,9},{9,1},{2,10},{10,2},{3,11},{11,3},{4,12},{12,4},... | collective-permute-start | bytes 2359304 | tf_op jit(solution)/shard_map/ppermute | solution.py:60
  93.7 2.3 collective-permute-start.5
  94.0 3.1 collective-permute-start.7
  304.5 5.7 %collective-permute-start.12 = (bf16[384,4096]{1,0:T(8,128)(2,1)S(1)}, bf16[384,4096]{1,0:T(8,128)(2,1)S(1)}, u32[]{:S(2)}, u32[]{:S(2)}) collective-permute-start(bf16[384,4096]{1,0:T(8,128)(2,1)S(1)} %convolution_convert_fusion.1), channel_id=1, source_target_pairs={{0,8},{8,0},{1,9},{9,1},{2,10},{10,2},{3,11},{11,3},{4,12},{12,4},... | collective-permute-start | bytes 9437192 | tf_op jit(solution)/shard_map/ppermute | solution.py:60
  312.2 6.4 %collective-permute-start.15 = (bf16[4,48,4096]{2,1,0:T(8,128)(2,1)S(1)}, bf16[4,48,4096]{2,1,0:T(8,128)(2,1)S(1)}, u32[]{:S(2)}, u32[]{:S(2)}) collective-permute-start(bf16[4,48,4096]{2,1,0:T(8,128)(2,1)S(1)} %pad_maximum_fusion), channel_id=1, source_target_pairs={{0,8},{8,0},{1,9},{9,1},{2,10},{10,2},{3,11},{11,3},{4,12},{12,4},... | collective-permute-start | bytes 4718600 | tf_op jit(solution)/shard_map/ppermute | solution.py:60
  312.4 6.2 %collective-permute-start.16 = (bf16[4,48,4096]{2,1,0:T(8,128)(2,1)S(1)}, bf16[4,48,4096]{2,1,0:T(8,128)(2,1)}, u32[]{:S(2)}, u32[]{:S(2)}) collective-permute-start(bf16[4,48,4096]{2,1,0:T(8,128)(2,1)S(1)} %collective-permute-done.11), channel_id=1, source_target_pairs={{0,8},{8,0},{1,9},{9,1},{2,10},{10,2},{3,11},{11,3},{4,12},{12,4},... | collective-permute-start | bytes 4718600 | tf_op jit(solution)/shard_map/ppermute | solution.py:60
  312.8 3.5 collective-permute-start.17
  316.5 13.2 %collective-permute-start.14 = (bf16[96,2048]{1,0:T(8,128)(2,1)S(1)}, bf16[96,2048]{1,0:T(8,128)(2,1)S(1)}, u32[]{:S(2)}, u32[]{:S(2)}) collective-permute-start(bf16[96,2048]{1,0:T(8,128)(2,1)S(1)} %get-tuple-element.86), channel_id=1, source_target_pairs={{32,0},{64,32},{96,64},{0,96},{33,1},{65,33},{97,65},{1,97},{34,2}... | collective-permute-start | bytes 1179656 | tf_op jit(solution)/shard_map/ppermute | solution.py:65
  317.4 12.3 %collective-permute-start.13 = (bf16[96,2048]{1,0:T(8,128)(2,1)S(1)}, bf16[96,2048]{1,0:T(8,128)(2,1)S(1)}, u32[]{:S(2)}, u32[]{:S(2)}) collective-permute-start(bf16[96,2048]{1,0:T(8,128)(2,1)S(1)} %get-tuple-element.87), channel_id=1, source_target_pairs={{96,0},{0,32},{32,64},{64,96},{97,1},{1,33},{33,65},{65,97},{98,2}... | collective-permute-start | bytes 1179656 | tf_op jit(solution)/shard_map/ppermute | solution.py:65
  333.1 5.7 %collective-permute-start.18 = (bf16[384,4096]{1,0:T(8,128)(2,1)S(1)}, bf16[384,4096]{1,0:T(8,128)(2,1)S(1)}, u32[]{:S(2)}, u32[]{:S(2)}) collective-permute-start(bf16[384,4096]{1,0:T(8,128)(2,1)S(1)} %convolution_convert_fusion), channel_id=1, source_target_pairs={{0,8},{8,0},{1,9},{9,1},{2,10},{10,2},{3,11},{11,3},{4,12},{12,4},... | collective-permute-start | bytes 9437192 | tf_op jit(solution)/shard_map/ppermute | solution.py:60
  333.2 5.1 %collective-permute-start.19 = (f32[17]{0:T(128)S(1)}, f32[17]{0:T(128)S(1)}, u32[]{:S(2)}, u32[]{:S(2)}) collective-permute-start(f32[17]{0:T(128)S(1)} %add.99), channel_id=1, source_target_pairs={{0,64},{32,96},{64,0},{96,32},{1,65},{33,97},{65,1},{97,33},{2,66}... | collective-permute-start | bytes 212 | tf_op jit(solution)/shard_map/ppermute | solution.py:60
  334.6 20.4 %collective-permute-start.25 = (bf16[96,4096]{1,0:T(8,128)(2,1)S(1)}, bf16[96,4096]{1,0:T(8,128)(2,1)S(1)}, u32[]{:S(2)}, u32[]{:S(2)}) collective-permute-start(bf16[96,4096]{1,0:T(8,128)(2,1)S(1)} %pad_maximum_fusion.6), channel_id=1, source_target_pairs={{32,0},{64,32},{96,64},{0,96},{33,1},{65,33},{97,65},{1,97},{34,2}... | collective-permute-start | bytes 2359304 | tf_op jit(solution)/shard_map/ppermute | solution.py:65
  336.4 21.7 %collective-permute-start.24 = (bf16[96,4096]{1,0:T(8,128)(2,1)S(1)}, bf16[96,4096]{1,0:T(8,128)(2,1)S(1)}, u32[]{:S(2)}, u32[]{:S(2)}) collective-permute-start(bf16[96,4096]{1,0:T(8,128)(2,1)S(1)} %pad_maximum_fusion.5), channel_id=1, source_target_pairs={{96,0},{0,32},{32,64},{64,96},{97,1},{1,33},{33,65},{65,97},{98,2}... | collective-permute-start | bytes 2359304 | tf_op jit(solution)/shard_map/ppermute | solution.py:65
  340.8 24.6 %collective-permute-start.20 = (bf16[96,2048]{1,0:T(8,128)(2,1)S(1)}, bf16[96,2048]{1,0:T(8,128)(2,1)S(1)}, u32[]{:S(2)}, u32[]{:S(2)}) collective-permute-start(bf16[96,2048]{1,0:T(8,128)(2,1)S(1)} %get-tuple-element.90), channel_id=1, source_target_pairs={{96,0},{0,32},{32,64},{64,96},{97,1},{1,33},{33,65},{65,97},{98,2}... | collective-permute-start | bytes 1179656 | tf_op jit(solution)/shard_map/ppermute | solution.py:65
  340.9 24.5 %collective-permute-start.22 = (bf16[96,2048]{1,0:T(8,128)(2,1)S(1)}, bf16[96,2048]{1,0:T(8,128)(2,1)S(1)}, u32[]{:S(2)}, u32[]{:S(2)}) collective-permute-start(bf16[96,2048]{1,0:T(8,128)(2,1)S(1)} %get-tuple-element.91), channel_id=1, source_target_pairs={{32,0},{64,32},{96,64},{0,96},{33,1},{65,33},{97,65},{1,97},{34,2}... | collective-permute-start | bytes 1179656 | tf_op jit(solution)/shard_map/ppermute | solution.py:65
  358.4 11.2 %collective-permute-start.26 = (bf16[48,4096]{1,0:T(8,128)(2,1)S(1)}, bf16[48,4096]{1,0:T(8,128)(2,1)S(1)}, u32[]{:S(2)}, u32[]{:S(2)}) collective-permute-start(bf16[48,4096]{1,0:T(8,128)(2,1)S(1)} %slice.193), channel_id=1, source_target_pairs={{0,16},{16,0},{1,17},{17,1},{2,18},{18,2},{3,19},{19,3},{4,20},{20... | collective-permute-start | bytes 1179656 | tf_op jit(solution)/shard_map/ppermute | solution.py:60
  366.7 20.0 %collective-permute-start.23 = (bf16[96,4096]{1,0:T(8,128)(2,1)}, bf16[96,4096]{1,0:T(8,128)(2,1)}, u32[]{:S(2)}, u32[]{:S(2)}) collective-permute-start(bf16[96,4096]{1,0:T(8,128)(2,1)} %pad_maximum_fusion.4), channel_id=1, source_target_pairs={{32,0},{64,32},{96,64},{0,96},{33,1},{65,33},{97,65},{1,97},{34,2}... | collective-permute-start | bytes 2359304 | tf_op jit(solution)/shard_map/ppermute | solution.py:65
  367.8 20.0 %collective-permute-start.21 = (bf16[96,4096]{1,0:T(8,128)(2,1)}, bf16[96,4096]{1,0:T(8,128)(2,1)}, u32[]{:S(2)}, u32[]{:S(2)}) collective-permute-start(bf16[96,4096]{1,0:T(8,128)(2,1)} %pad_maximum_fusion.3), channel_id=1, source_target_pairs={{96,0},{0,32},{32,64},{64,96},{97,1},{1,33},{33,65},{65,97},{98,2}... | collective-permute-start | bytes 2359304 | tf_op jit(solution)/shard_map/ppermute | solution.py:65
  370.7 11.4 %all-to-all-start.2 = ((bf16[8,48,512]{2,1,0:T(8,128)(2,1)}), bf16[8,48,512]{2,1,0:T(8,128)(2,1)S(1)}, u32[]{:S(2)}, u32[]{:S(2)}) async-start(bf16[8,48,512]{2,1,0:T(8,128)(2,1)} %copy.80), calls=%async_computation.2 | async-start | bytes 786432 | tf_op jit(solution)/shard_map/all_to_all | solution.py:56
  374.2 5.2 %collective-permute-start.27 = (f32[17]{0:T(128)S(1)}, f32[17]{0:T(128)S(1)}, u32[]{:S(2)}, u32[]{:S(2)}) collective-permute-start(f32[17]{0:T(128)S(1)} %add.101), channel_id=1, source_target_pairs={{0,16},{16,0},{1,17},{17,1},{2,18},{18,2},{3,19},{19,3},{4,20},{20... | collective-permute-start | bytes 212 | tf_op jit(solution)/shard_map/ppermute | solution.py:60
  379.4 4.7 %collective-permute-start.28 = (f32[17]{0:T(128)S(1)}, f32[17]{0:T(128)S(1)}, u32[]{:S(2)}, u32[]{:S(2)}) collective-permute-start(f32[17]{0:T(128)S(1)} %add.111), channel_id=1, source_target_pairs={{0,8},{8,0},{1,9},{9,1},{2,10},{10,2},{3,11},{11,3},{4,12},{12,4},... | collective-permute-start | bytes 212 | tf_op jit(solution)/shard_map/ppermute | solution.py:60
  389.5 10.7 %collective-permute-start.29 = (bf16[48,4096]{1,0:T(8,128)(2,1)S(1)}, bf16[48,4096]{1,0:T(8,128)(2,1)S(1)}, u32[]{:S(2)}, u32[]{:S(2)}) collective-permute-start(bf16[48,4096]{1,0:T(8,128)(2,1)S(1)} %slice.177), channel_id=1, source_target_pairs={{0,16},{16,0},{1,17},{17,1},{2,18},{18,2},{3,19},{19,3},{4,20},{20... | collective-permute-start | bytes 1179656 | tf_op jit(solution)/shard_map/ppermute | solution.py:60
  (13 other events, 561.6 us)
